TPU v7x, 256 devices: a whole 4x4x8 slice. The times are simulated.
256 devices in a mesh: row: 16 (over z_lo, x, core), col: 16 (over z_hi, y).
Axes of the slice: x: 4, y: 4, z: 8 (z_hi: 4, z_lo: 2; z = z_hi * 2 + z_lo), core: 2. Of those that a mesh axis runs over, the one named last changes fastest.
Arguments:
- hamiltonian: bfloat16 [4096, 4096], P('row', 'col'), may hold values from -9 to 9
- density: bfloat16 [4096, 4096], P('row', 'col'), may hold values from -9 to 9
- pattern: int32 [16, 16], P('row', 'col'), may hold values from 0 to 1, as said below
Outputs:
- gradient: float32 [4096, 4096], P('row', 'col')
- final_density: bfloat16 [4096, 4096], P('row', 'col')
Inputs may be any that keep to these rules, and one draw needn't show every extreme that they name: pattern is symmetric and its diagonal is all ones.
All inputs are finite; a program needn't handle non-finite values.
Results may differ from a plain program's by a relative error of at most 0.0053.
Values may be sent and summed in bfloat16 or wider, within the bound.
No kernel may reach another device: no remote copies, remote signals or barrier semaphores. Data moves between devices by JAX's collectives and lax.ppermute only.
A program may use at most 64 MiB of HBM per device.

v0:
```python
import jax
import jax.numpy as jnp
from jax import lax
from jax.sharding import PartitionSpec as P

STEPS = 2


step_rate = 0.1


def apply_pattern(entries, pattern):
    row_tiles, col_tiles = pattern.shape
    tile_size = entries.shape[0] // row_tiles
    shaped = (
        entries.reshape(row_tiles, tile_size, col_tiles, tile_size)
        * pattern.astype(entries.dtype)[:, None, :, None]
    )
    return shaped.reshape(entries.shape)


def local(hamiltonian, density, pattern):
    ham_masked = apply_pattern(hamiltonian, pattern)
    dens_masked = apply_pattern(density, pattern)
    local_cols = ham_masked.shape[1]
    ham_rows = lax.all_gather(ham_masked, "col", axis=1, tiled=True)
    scaling = 1.0 / jnp.sqrt(jnp.float32(ham_rows.shape[1]))
    empty_sum = jnp.zeros(ham_masked.shape, jnp.float32)
    gradient = empty_sum
    for iteration in range(STEPS):
        forward = jnp.dot(
            ham_rows,
            lax.all_gather(dens_masked, "row", axis=0, tiled=True),
            preferred_element_type=jnp.float32,
        )
        product = apply_pattern(forward * scaling, pattern).astype(jnp.bfloat16)
        prod_cols = lax.all_gather(product, "row", axis=0, tiled=True)
        triple_sum = jnp.dot(
            lax.all_gather(dens_masked, "col", axis=1, tiled=True),
            prod_cols,
            preferred_element_type=jnp.float32,
        )
        whole_rows = lax.all_gather(product, "col", axis=1, tiled=True)
        turned = lax.all_to_all(whole_rows.T, "row", split_axis=0, concat_axis=1, tiled=True)
        col_start = lax.axis_index("col") * local_cols
        mirror = lax.dynamic_slice_in_dim(turned, col_start, local_cols, 1)
        triple = apply_pattern(triple_sum * scaling, pattern)
        gradient = product.astype(jnp.float32) + mirror.astype(jnp.float32) - 2.0 * triple
        dens_masked = (dens_masked.astype(jnp.float32) - step_rate * gradient).astype(jnp.bfloat16)
    return (gradient, dens_masked)


def solution(mesh):
    return jax.shard_map(
        local,
        mesh=mesh,
        in_specs=(P("row", "col"), P("row", "col"), P("row", "col")),
        out_specs=(P("row", "col"), P("row", "col")),
        check_vma=False,
    )
```

profile of v0, /device:TPU:1, one launch (start us, length us, event | category | flops | bytes accessed | tf_op | source)
XLA Modules:
  0.0 501.9 jit_solution(15771055166093653170)
XLA Ops:
  7.9 1.6 broadcast_multiply_fusion
  9.5 1.6 broadcast_multiply_fusion.1
  11.2 40.1 %all-gather.12.cloned.1.call-done = bf16[4096,256]{1,0:T(8,128)(2,1)} async-done(((bf16[256,256]{1,0:T(8,128)(2,1)}), bf16[4096,256]{1,0:T(8,128)(2,1)}) %all-gather.12.cloned.1.call-update) | async-done | bytes 2097168 | tf_op jit(solution)/shard_map/all_gather | solution.py:33
  51.3 65.1 %all-gather.10.cloned.1.call-done = bf16[256,4096]{1,0:T(8,128)(2,1)} async-done(((bf16[256,256]{1,0:T(8,128)(2,1)}), bf16[256,4096]{1,0:T(8,128)(2,1)}) %all-gather.10.cloned.1.call-update) | async-done | bytes 2097168 | tf_op jit(solution)/shard_map/all_gather | solution.py:26
  116.4 3.6 fusion.6
  120.6 59.9 %all-gather.14.cloned.1.call-done = bf16[256,4096]{1,0:T(8,128)(2,1)} async-done(((bf16[256,256]{1,0:T(8,128)(2,1)}), bf16[256,4096]{1,0:T(8,128)(2,1)}) %all-gather.14.cloned.1.call-update) | async-done | bytes 2097168 | tf_op jit(solution)/shard_map/all_gather | solution.py:43
  180.5 3.2 copy.20
  183.7 5.5 %all-to-all-start = ((bf16[16,256,256]{1,2,0:T(8,128)(2,1)}), bf16[16,256,256]{1,2,0:T(8,128)(2,1)S(1)}, u32[]{:S(2)}, u32[]{:S(2)}) async-start(bf16[16,256,256]{1,2,0:T(8,128)(2,1)} %bitcast.25), calls=%async_computation | async-start | bytes 4194304 | tf_op jit(solution)/shard_map/all_to_all | solution.py:44
  189.3 0.5 all-gather.18.cloned.1.call-update
  189.9 30.7 %all-to-all-done = bf16[16,256,256]{1,2,0:T(8,128)(2,1)S(1)} async-done(((bf16[16,256,256]{1,2,0:T(8,128)(2,1)}), bf16[16,256,256]{1,2,0:T(8,128)(2,1)S(1)}, u32[]{:S(2)}, u32[]{:S(2)}) %all-to-all-start) | async-done | bytes 2097184 | tf_op jit(solution)/shard_map/all_to_all | solution.py:44
  220.6 25.6 %all-gather.16.cloned.1.call-done = bf16[256,4096]{1,0:T(8,128)(2,1)} async-done(((bf16[256,256]{1,0:T(8,128)(2,1)}), bf16[256,4096]{1,0:T(8,128)(2,1)}) %all-gather.16.cloned.1.call-update) | async-done | bytes 2097168 | tf_op jit(solution)/shard_map/all_gather | solution.py:39
  246.2 37.0 %all-gather.18.cloned.1.call-done = bf16[4096,256]{1,0:T(8,128)(2,1)} async-done(((bf16[256,256]{1,0:T(8,128)(2,1)}), bf16[4096,256]{1,0:T(8,128)(2,1)}) %all-gather.18.cloned.1.call-update) | async-done | bytes 2097168 | tf_op jit(solution)/shard_map/all_gather | solution.py:37
  283.2 3.6 fusion.8
  286.9 36.5 %all-gather.20.cloned.1.call-done = bf16[4096,256]{1,0:T(8,128)(2,1)} async-done(((bf16[256,256]{1,0:T(8,128)(2,1)}), bf16[4096,256]{1,0:T(8,128)(2,1)}) %all-gather.20.cloned.1.call-update) | async-done | bytes 2097168 | tf_op jit(solution)/shard_map/all_gather | solution.py:33
  323.4 3.0 fusion.7
  326.4 0.7 all-gather.24.cloned.1.call-update
  327.1 61.5 %all-gather.22.cloned.1.call-done = bf16[256,4096]{1,0:T(8,128)(2,1)} async-done(((bf16[256,256]{1,0:T(8,128)(2,1)}), bf16[256,4096]{1,0:T(8,128)(2,1)}) %all-gather.22.cloned.1.call-update) | async-done | bytes 2097168 | tf_op jit(solution)/shard_map/all_gather | solution.py:43
  388.6 3.2 copy.19
  391.8 5.5 %all-to-all-start.1 = ((bf16[16,256,256]{1,2,0:T(8,128)(2,1)}), bf16[16,256,256]{1,2,0:T(8,128)(2,1)S(1)}, u32[]{:S(2)}, u32[]{:S(2)}) async-start(bf16[16,256,256]{1,2,0:T(8,128)(2,1)} %bitcast.24), calls=%async_computation.1 | async-start | bytes 4194304 | tf_op jit(solution)/shard_map/all_to_all | solution.py:44
  397.4 0.7 all-gather.26.cloned.1.call-update
  398.1 30.6 %all-to-all-done.1 = bf16[16,256,256]{1,2,0:T(8,128)(2,1)S(1)} async-done(((bf16[16,256,256]{1,2,0:T(8,128)(2,1)}), bf16[16,256,256]{1,2,0:T(8,128)(2,1)S(1)}, u32[]{:S(2)}, u32[]{:S(2)}) %all-to-all-start.1) | async-done | bytes 2097184 | tf_op jit(solution)/shard_map/all_to_all | solution.py:44
  428.8 25.7 %all-gather.24.cloned.1.call-done = bf16[256,4096]{1,0:T(8,128)(2,1)} async-done(((bf16[256,256]{1,0:T(8,128)(2,1)}), bf16[256,4096]{1,0:T(8,128)(2,1)}) %all-gather.24.cloned.1.call-update) | async-done | bytes 2097168 | tf_op jit(solution)/shard_map/all_gather | solution.py:39
  454.5 37.2 %all-gather.26.cloned.1.call-done = bf16[4096,256]{1,0:T(8,128)(2,1)} async-done(((bf16[256,256]{1,0:T(8,128)(2,1)}), bf16[4096,256]{1,0:T(8,128)(2,1)}) %all-gather.26.cloned.1.call-update) | async-done | bytes 2097168 | tf_op jit(solution)/shard_map/all_gather | solution.py:37
  491.7 3.7 subtract_convert_fusion
  (29 shorter events, 1.2 us)
Async XLA Ops:
  7.2 44.1 %all-gather.12.cloned.1.call-start = ((), (), s32[]{:S(2)}) async-start(), calls=%async_computation.3 | async-start | bytes 2228224 | tf_op jit(solution)/shard_map/all_gather | solution.py:33
  9.5 106.9 %all-gather.10.cloned.1.call-start = ((), (), s32[]{:S(2)}) async-start(), calls=%async_computation.2 | async-start | bytes 2228224 | tf_op jit(solution)/shard_map/all_gather | solution.py:26
  11.1 169.4 %all-gather.14.cloned.1.call-start = ((), (), s32[]{:S(2)}) async-start(), calls=%async_computation.4 | async-start | bytes 2228224 | tf_op jit(solution)/shard_map/all_gather | solution.py:43
  120.0 126.2 %all-gather.16.cloned.1.call-start = ((), (), s32[]{:S(2)}) async-start(), calls=%async_computation.5 | async-start | bytes 2228224 | tf_op jit(solution)/shard_map/all_gather | solution.py:39
  183.7 99.5 %copy-start = (bf16[256,256]{1,0:T(8,128)(2,1)S(1)}, bf16[256,256]{1,0:T(8,128)(2,1)}, u32[]{:S(2)}) copy-start(bf16[256,256]{1,0:T(8,128)(2,1)} %broadcast_multiply_fusion) | copy-start | bytes 393220
  183.7 99.5 %copy-start.2 = (bf16[256,256]{1,0:T(8,128)(2,1)S(1)}, bf16[256,256]{1,0:T(8,128)(2,1)}, u32[]{:S(2)}) copy-start(bf16[256,256]{1,0:T(8,128)(2,1)} %fusion.6) | copy-start | bytes 393220
  183.7 36.8 %all-to-all-start = ((bf16[16,256,256]{1,2,0:T(8,128)(2,1)}), bf16[16,256,256]{1,2,0:T(8,128)(2,1)S(1)}, u32[]{:S(2)}, u32[]{:S(2)}) async-start(bf16[16,256,256]{1,2,0:T(8,128)(2,1)} %bitcast.25), calls=%async_computation | async-start | bytes 4194304 | tf_op jit(solution)/shard_map/all_to_all | solution.py:44
  189.2 94.0 %all-gather.18.cloned.1.call-start = ((), (), s32[]{:S(2)}) async-start(), calls=%async_computation.6 | async-start | bytes 2228224 | tf_op jit(solution)/shard_map/all_gather | solution.py:37
  189.8 133.6 %all-gather.20.cloned.1.call-start = ((), (), s32[]{:S(2)}) async-start(), calls=%async_computation.7 | async-start | bytes 2228224 | tf_op jit(solution)/shard_map/all_gather | solution.py:33
  220.6 102.8 %copy-start.4 = (bf16[256,4096]{1,0:T(8,128)(2,1)S(1)}, bf16[256,4096]{1,0:T(8,128)(2,1)}, u32[]{:S(2)}) copy-start(bf16[256,4096]{1,0:T(8,128)(2,1)} %all-gather.10.cloned.1.call-done) | copy-start | bytes 6291460
  286.8 101.8 %all-gather.22.cloned.1.call-start = ((), (), s32[]{:S(2)}) async-start(), calls=%async_computation.8 | async-start | bytes 2228224 | tf_op jit(solution)/shard_map/all_gather | solution.py:43
  326.4 128.1 %all-gather.24.cloned.1.call-start = ((), (), s32[]{:S(2)}) async-start(), calls=%async_computation.9 | async-start | bytes 2228224 | tf_op jit(solution)/shard_map/all_gather | solution.py:39
  391.8 99.8 %copy-start.1 = (bf16[256,256]{1,0:T(8,128)(2,1)S(1)}, bf16[256,256]{1,0:T(8,128)(2,1)}, u32[]{:S(2)}) copy-start(bf16[256,256]{1,0:T(8,128)(2,1)} %fusion.8) | copy-start | bytes 393220
  391.8 99.8 %copy-start.3 = (bf16[256,256]{1,0:T(8,128)(2,1)S(1)}, bf16[256,256]{1,0:T(8,128)(2,1)}, u32[]{:S(2)}) copy-start(bf16[256,256]{1,0:T(8,128)(2,1)} %fusion.7) | copy-start | bytes 393220
  391.8 36.8 %all-to-all-start.1 = ((bf16[16,256,256]{1,2,0:T(8,128)(2,1)}), bf16[16,256,256]{1,2,0:T(8,128)(2,1)S(1)}, u32[]{:S(2)}, u32[]{:S(2)}) async-start(bf16[16,256,256]{1,2,0:T(8,128)(2,1)} %bitcast.24), calls=%async_computation.1 | async-start | bytes 4194304 | tf_op jit(solution)/shard_map/all_to_all | solution.py:44
  397.4 94.3 %all-gather.26.cloned.1.call-start = ((), (), s32[]{:S(2)}) async-start(), calls=%async_computation.10 | async-start | bytes 2228224 | tf_op jit(solution)/shard_map/all_gather | solution.py:37
Sparse Core Ops, SparseCore 0:
  10.4 40.8 all-gather.11
  54.2 62.0 all-gather.9
  120.1 60.3 all-gather.13
  183.3 62.8 all-gather.15
  248.5 34.6 all-gather.17
  287.0 36.4 all-gather.19
  326.5 62.0 all-gather.21
  391.6 62.8 all-gather.23
  456.9 34.6 all-gather.25
where the time goes:
time: 502 us
  waiting for transfers between devices  452 us (90%)
  between operations  14.5 us (3%)
  matrix products  13.8 us (3%)
  starting transfers between devices  11.4 us (2%)
  local copies, waits for them, and re-layouts  6.62 us (1%)
    all_gather x2, waiting for transfers between devices, local(): whole_rows = lax.all_gather(product, 'col', axis=1, tiled=True)  121 us
    all_gather x2, waiting for transfers between devices, local(): lax.all_gather(dens_masked, 'row', axis=0, tiled=True)  76.6 us
    all_gather x2, waiting for transfers between devices, local(): prod_cols = lax.all_gather(product, 'row', axis=0, tiled=True)  74.1 us
    all_gather x1, waiting for transfers between devices, local(): ham_rows = lax.all_gather(ham_masked, 'col', axis=1, tiled=True)  65.1 us
    all_to_all x2, waiting for transfers between devices, local(): lax.all_to_all(whole_rows.T, 'row', split_axis=0, concat_axis=1, tiled=True)  61.2 us
    all_gather x2, waiting for transfers between devices, local(): lax.all_gather(dens_masked, 'col', axis=1, tiled=True)  51.3 us
    all_to_all x2, starting transfers between devices, local(): lax.all_to_all(whole_rows.T, 'row', split_axis=0, concat_axis=1, tiled=True)  11.1 us
  transfers between devices with their start and end apart: 11, of which 11 were waited for; matrix products, arithmetic and copies ran while one was open for 2% of the time, Pallas kernels for 0%

commit v1 on v0

v1 whole, which is shorter than its diff:
```python
import itertools

import jax
import jax.numpy as jnp
from jax import lax
from jax.experimental import pallas as pl
from jax.experimental.pallas import tpu as pltpu
from jax.sharding import Mesh
from jax.sharding import PartitionSpec as P

STEPS = 2
RATE = 0.1
ROW = ("zlo", "x", "core")
COL = ("zhi", "y")
SIZES = {"zlo": 2, "x": 4, "core": 2, "zhi": 4, "y": 4}
FIRST = ((0, 2, 3, 1), (2, 0, 1, 3))
VMEM = pl.BlockSpec(memory_space=pltpu.VMEM)
SMEM = pl.BlockSpec(memory_space=pltpu.SMEM)
F32, BF16 = jnp.float32, jnp.bfloat16
BLOCK = jax.ShapeDtypeStruct((256, 256), BF16)
BLOCK32 = jax.ShapeDtypeStruct((256, 256), F32)


def fetch(value, **offsets):
    axes = tuple(offsets)
    sizes = [SIZES[a] for a in axes]
    pairs = []
    for place in itertools.product(*[range(n) for n in sizes]):
        source = dest = 0
        for here, size, a in zip(place, sizes, axes):
            source = source * size + (here + offsets[a]) % size
            dest = dest * size + here
        pairs.append((source, dest))
    return lax.ppermute(value, axes, pairs)


def transposed(value):
    return lax.ppermute(value, ROW + COL, [(16 * i + j, 16 * j + i) for i in range(16) for j in range(16)])


def after(value, *others):
    return lax.optimization_barrier((value, *others))[0]


def call(kernel, outs, args, name, megabytes=4, flops=0):
    moved = sum(a.size * a.dtype.itemsize for a in args) + sum(o.size * o.dtype.itemsize for o in outs)
    return pl.pallas_call(
        kernel,
        out_shape=outs,
        in_specs=[SMEM if a.dtype == jnp.int32 else VMEM for a in args],
        out_specs=[VMEM] * len(outs),
        compiler_params=pltpu.CompilerParams(vmem_limit_bytes=megabytes << 20),
        cost_estimate=pl.CostEstimate(flops=flops, bytes_accessed=moved, transcendentals=0),
        name=name,
    )(*args)


def mask_kernel(keep_ref, ham_ref, dens_ref, ham_out, dens_out):
    keep = keep_ref[0, 0].astype(F32)
    ham_out[...] = (ham_ref[...].astype(F32) * keep).astype(BF16)
    dens_out[...] = (dens_ref[...].astype(F32) * keep).astype(BF16)


def pack_kernel(*refs):
    for n, ref in enumerate(refs[:-1]):
        refs[-1][n] = ref[...]


def pack(blocks):
    return call(pack_kernel, [jax.ShapeDtypeStruct((len(blocks), 256, 256), BF16)], blocks, "pack")[0]


def multiply_kernel(at_ref, *refs):
    panel, (held_ref, swapped_ref, mine_ref, other_ref) = refs[:-4], refs[-4:]
    acc = jnp.zeros((512, 256), F32)
    for n, ref in enumerate(panel):
        place = at_ref[2 * n]
        block = jnp.where(at_ref[2 * n + 1] == 0, held_ref[place], swapped_ref[place])
        acc += jnp.dot(ref[...].reshape(512, 256), block, preferred_element_type=F32)
    acc = acc * (1.0 / 64.0)
    first, second = acc[:256], acc[256:]
    mine_first = at_ref[16] == 0
    mine_ref[...] = jnp.where(mine_first, first, second)
    other_ref[...] = jnp.where(mine_first, second, first).astype(BF16)


def multiply(at, panel, columns):
    return call(multiply_kernel, [BLOCK32, BLOCK], [at, *panel, *columns], "multiply", 12, 2 * 4096 * 256 * 256)


def product_kernel(keep_ref, mine_ref, other_ref, out_ref):
    out_ref[...] = ((mine_ref[...] + other_ref[...].astype(F32)) * keep_ref[0, 0].astype(F32)).astype(BF16)


def update_kernel(keep_ref, mine_ref, other_ref, prod_ref, turned_ref, dens_ref, *outs):
    triple = (mine_ref[...] + other_ref[...].astype(F32)) * keep_ref[0, 0].astype(F32)
    gradient = prod_ref[...].astype(F32) + turned_ref[...].T.astype(F32) - 2.0 * triple
    outs[0][...] = (dens_ref[...].astype(F32) - RATE * gradient).astype(BF16)
    if len(outs) == 2:
        outs[1][...] = gradient


PANEL = ((0, 0), (0, 1), (1, 0), (1, 1), (3, 0), (3, 1), (2, 0), (2, 1))
AROUND = (0, 1, 3, 2)


def start_z(block, ms):
    pieces = []
    for m in ms:
        pairs = []
        for zlo in range(2):
            for zhi in range(4):
                source = 4 * zlo + (FIRST[zlo][zhi] ^ m)
                pairs.append(((source % 2) * 4 + source // 2, zlo * 4 + zhi))
        pieces.append(lax.ppermute(block, ("zlo", "zhi"), pairs))
    return pieces


def gather_panel(block):
    z = start_z(block, range(4))
    a, b = pack(z[:2]), pack(z[2:])
    up_a, down_a = fetch(a, y=1), fetch(a, y=3)
    up_b, down_b = fetch(b, y=1), fetch(b, y=3)
    return [a, b, up_a, up_b, down_a, down_b, fetch(up_a, y=1), fetch(down_b, y=3)]


def gather_x(block):
    held = pack([block, fetch(block, x=1), fetch(block, x=3), fetch(block, x=2)])
    return [held, fetch(held, core=1)]


def places():
    zlo, x, core, zhi, y = (lax.axis_index(a) for a in ROW + COL)
    first = jnp.take(jnp.array(FIRST, jnp.int32).reshape(-1), zlo * 4 + zhi)
    rows = []
    for dy, pair in PANEL:
        column = (y + dy) % 4
        dx = ((pair ^ (first // 2)) * 2 + column // 2 - x) % 4
        rows += [jnp.where(dx == 0, 0, jnp.where(dx == 1, 1, jnp.where(dx == 3, 2, 3))), (column % 2) ^ core]
    rows.append((first % 2) ^ zlo)
    return jnp.stack(rows).astype(jnp.int32)


def local(hamiltonian, density, pattern):
    at = places()
    ham, dens = call(mask_kernel, [BLOCK, BLOCK], [pattern, hamiltonian, density], "mask")
    ham_panel = gather_panel(ham)
    for step in range(STEPS):
        last = step == STEPS - 1
        dens_cols = gather_x(dens)
        dens_panel = gather_panel(dens)
        mine, other = multiply(at, ham_panel, dens_cols)
        product = call(product_kernel, [BLOCK], [pattern, mine, fetch(other, zlo=1)], "product")[0]
        prod_cols = gather_x(product)
        turned = transposed(product)
        mine, other = multiply(at, dens_panel, prod_cols)
        outs = call(
            update_kernel,
            [BLOCK, BLOCK32] if last else [BLOCK],
            [pattern, mine, fetch(other, zlo=1), product, turned, dens],
            "update",
        )
        dens = outs[0]
    return outs[1], dens


def solution(mesh):
    fine = Mesh(mesh.devices.reshape(2, 4, 2, 4, 4), ROW + COL)
    return jax.shard_map(
        local,
        mesh=fine,
        in_specs=(P(ROW, COL), P(ROW, COL), P(ROW, COL)),
        out_specs=(P(ROW, COL), P(ROW, COL)),
        check_vma=False,
    )
```

time: 502 us -> 175 us (0.35)
  waiting for transfers between devices: 452 us -> 54.1 us
  starting transfers between devices: 11.4 us -> 107 us
  matrix products: 13.8 us -> 0 us
  between operations: 14.5 us -> 2.64 us
  Pallas kernels: 0 us -> 6.48 us
    all_gather x9 -> x0, waiting for transfers between devices: 389 us -> none  [the longest x2 121 us: local(): whole_rows = lax.all_gather(product, 'col', axis=1, tiled=True)]
    ppermute x0 -> x52, starting transfers between devices: none -> 107 us  [the longest x38 72.3 us: fetch(): return lax.ppermute(value, axes, pairs)]
    all_to_all x2 -> x0, waiting for transfers between devices: 61.2 us -> none  [local(): lax.all_to_all(whole_rows.T, 'row', split_axis=0, concat_axis=1, tiled=True)]
    ppermute x0 -> x52, waiting for transfers between devices: none -> 54.1 us  [the longest x38 45.1 us: fetch(): return lax.ppermute(value, axes, pairs)]
    dot_general x4 -> x0, matrix products: 13.8 us -> none  [the longest x2 7.28 us: local(): jnp.dot(lax.all_gather(dens_masked, 'col', axis=1, tiled=True), prod_cols...]
    all_to_all x2 -> x0, starting transfers between devices: 11.1 us -> none  [local(): lax.all_to_all(whole_rows.T, 'row', split_axis=0, concat_axis=1, tiled=True)]
    pallas_call x0 -> x19, Pallas kernels: none -> 6.48 us  [call(): pl.pallas_call(kernel, out_shape=outs, in_specs=[SMEM if a.dtype == jnp.i...]
    all_to_all x2 -> x0, local copies, waits for them, and re-layouts: 6.39 us -> none  [local(): lax.all_to_all(whole_rows.T, 'row', split_axis=0, concat_axis=1, tiled=True)]
  transfers between devices with their start and end apart: 11 -> 52, of which waited for: 11 -> 18; matrix products, arithmetic and copies ran while one was open for 2% -> 0% of each run, Pallas kernels for 0% -> 2%
where the time goes in v1:
time: 175 us; the launch traced here: 173 us
  starting transfers between devices  107 us (61%)
  waiting for transfers between devices  54.1 us (31%)
  Pallas kernels  6.48 us (4%)
  local copies, waits for them, and re-layouts  3.13 us (2%)
  between operations  2.64 us (2%)
    ppermute x38, starting transfers between devices, fetch(): return lax.ppermute(value, axes, pairs)  72.3 us
    ppermute x38, waiting for transfers between devices, fetch(): return lax.ppermute(value, axes, pairs)  45.1 us
    ppermute x12, starting transfers between devices, start_z(): pieces.append(lax.ppermute(block, ('zlo', 'zhi'), pairs))  29.3 us
    ppermute x12, waiting for transfers between devices, start_z(): pieces.append(lax.ppermute(block, ('zlo', 'zhi'), pairs))  9.04 us
    pallas_call x19, Pallas kernels, call(): pl.pallas_call(kernel, out_shape=outs, in_specs=[SMEM if a.dtype == jnp.i...  6.48 us
    ppermute x2, starting transfers between devices, transposed(): lax.ppermute(value, ROW + COL, [(16 * i + j, 16 * j + i) for i in range(1...  5.47 us
  transfers between devices with their start and end apart: 52, of which 18 were waited for; matrix products, arithmetic and copies ran while one was open for 0% of the time, Pallas kernels for 2%

profile of v1, /device:TPU:1, one launch (start us, length us, event | category | flops | bytes accessed | tf_op | source)
XLA Modules:
  0.0 173.4 jit_solution(10780196315071608219)
XLA Ops:
  3.1 3.4 %collective-permute-start.20 = (bf16[256,256]{1,0:T(8,128)(2,1)S(1)}, bf16[256,256]{1,0:T(8,128)(2,1)S(1)}, u32[]{:S(2)}, u32[]{:S(2)}) collective-permute-start(bf16[256,256]{1,0:T(8,128)(2,1)S(1)} %get-tuple-element.14.refs_0_.dens_ref), channel_id=1, source_target_pairs={{32,0},{64,32},{96,64},{0,96},{33,1},{65,33},{97,65},{1,97},{34,2}... | collective-permute-start | bytes 393224 | tf_op jit(solution)/shard_map/ppermute | solution.py:34
  8.9 7.3 %collective-permute-start.11 = (bf16[256,256]{1,0:T(8,128)(2,1)S(1)}, bf16[256,256]{1,0:T(8,128)(2,1)S(1)}, u32[]{:S(2)}, u32[]{:S(2)}) collective-permute-start(bf16[256,256]{1,0:T(8,128)(2,1)S(1)} %get-tuple-element.15), channel_id=1, source_target_pairs={{128,0},{132,4},{4,8},{0,12},{140,128},{136,132},{8,136},{12,140},... | collective-permute-start | bytes 393224 | tf_op jit(solution)/shard_map/ppermute | solution.py:115
  17.4 4.3 %collective-permute-start.13 = (bf16[256,256]{1,0:T(8,128)(2,1)S(1)}, bf16[256,256]{1,0:T(8,128)(2,1)S(1)}, u32[]{:S(2)}, u32[]{:S(2)}) collective-permute-start(bf16[256,256]{1,0:T(8,128)(2,1)S(1)} %get-tuple-element.15), channel_id=1, source_target_pairs={{132,0},{128,4},{0,8},{4,12},{136,128},{140,132},{12,136},{8,140},... | collective-permute-start | bytes 393224 | tf_op jit(solution)/shard_map/ppermute | solution.py:115
  24.2 3.9 %collective-permute-done.11.refs_1_ = bf16[256,256]{1,0:T(8,128)(2,1)S(1)} collective-permute-done((bf16[256,256]{1,0:T(8,128)(2,1)S(1)}, bf16[256,256]{1,0:T(8,128)(2,1)S(1)}, u32[]{:S(2)}, u32[]{:S(2)}) %collective-permute-start.11) | collective-permute-done | bytes 131104 | tf_op jit(solution)/shard_map/ppermute | solution.py:115
  34.3 3.6 %collective-permute-start.18 = (bf16[2,256,256]{2,1,0:T(8,128)(2,1)S(1)}, bf16[2,256,256]{2,1,0:T(8,128)(2,1)S(1)}, u32[]{:S(2)}, u32[]{:S(2)}) collective-permute-start(bf16[2,256,256]{2,1,0:T(8,128)(2,1)S(1)} %collective-permute-done.14.refs_2_), channel_id=1, source_target_pairs={{1,0},{2,1},{3,2},{0,3},{5,4},{6,5},{7,6},{4,7},{9,8},{10,9},{11,1... | collective-permute-start | bytes 786440 | tf_op jit(solution)/shard_map/ppermute | solution.py:34
  40.3 3.0 %collective-permute-done.16.refs_4_ = bf16[2,256,256]{2,1,0:T(8,128)(2,1)S(1)} collective-permute-done((bf16[2,256,256]{2,1,0:T(8,128)(2,1)S(1)}, bf16[2,256,256]{2,1,0:T(8,128)(2,1)S(1)}, u32[]{:S(2)}, u32[]{:S(2)}) %collective-permute-start.16) | collective-permute-done | bytes 262176 | tf_op jit(solution)/shard_map/ppermute | solution.py:34
  45.7 3.2 %collective-permute-done.19.refs_7_ = bf16[2,256,256]{2,1,0:T(8,128)(2,1)S(1)} collective-permute-done((bf16[2,256,256]{2,1,0:T(8,128)(2,1)S(1)}, bf16[2,256,256]{2,1,0:T(8,128)(2,1)S(1)}, u32[]{:S(2)}, u32[]{:S(2)}) %collective-permute-start.19) | collective-permute-done | bytes 262176 | tf_op jit(solution)/shard_map/ppermute | solution.py:34
  50.2 7.4 %collective-permute-start.24 = (bf16[256,256]{1,0:T(8,128)(2,1)S(1)}, bf16[256,256]{1,0:T(8,128)(2,1)S(1)}, u32[]{:S(2)}, u32[]{:S(2)}) collective-permute-start(bf16[256,256]{1,0:T(8,128)(2,1)S(1)} %get-tuple-element.17), channel_id=1, source_target_pairs={{128,0},{0,128},{129,1},{1,129},{130,2},{2,130},{131,3},{3,131},{1... | collective-permute-start | bytes 393224 | tf_op jit(solution)/shard_map/ppermute | solution.py:34
  57.6 4.3 %collective-permute-start.3 = (bf16[256,256]{1,0:T(8,128)(2,1)S(1)}, bf16[256,256]{1,0:T(8,128)(2,1)S(1)}, u32[]{:S(2)}, u32[]{:S(2)}) collective-permute-start(bf16[256,256]{1,0:T(8,128)(2,1)S(1)} %get-tuple-element.14.refs_0_.dens_ref), channel_id=1, source_target_pairs={{132,0},{128,4},{0,8},{4,12},{136,128},{140,132},{12,136},{8,140},... | collective-permute-start | bytes 393224 | tf_op jit(solution)/shard_map/ppermute | solution.py:115
  62.6 3.0 %collective-permute-start.1 = (bf16[256,256]{1,0:T(8,128)(2,1)S(1)}, bf16[256,256]{1,0:T(8,128)(2,1)S(1)}, u32[]{:S(2)}, u32[]{:S(2)}) collective-permute-start(bf16[256,256]{1,0:T(8,128)(2,1)S(1)} %get-tuple-element.14.refs_0_.dens_ref), channel_id=1, source_target_pairs={{128,0},{132,4},{4,8},{0,12},{140,128},{136,132},{8,136},{12,140},... | collective-permute-start | bytes 393224 | tf_op jit(solution)/shard_map/ppermute | solution.py:115
  83.7 3.7 %collective-permute-done.5.refs_3_ = bf16[2,256,256]{2,1,0:T(8,128)(2,1)S(1)} collective-permute-done((bf16[2,256,256]{2,1,0:T(8,128)(2,1)S(1)}, bf16[2,256,256]{2,1,0:T(8,128)(2,1)S(1)}, u32[]{:S(2)}, u32[]{:S(2)}) %collective-permute-start.5) | collective-permute-done | bytes 262176 | tf_op jit(solution)/shard_map/ppermute | solution.py:34
  87.3 3.1 %collective-permute-start.30 = (bf16[256,256]{1,0:T(8,128)(2,1)S(1)}, bf16[256,256]{1,0:T(8,128)(2,1)S(1)}, u32[]{:S(2)}, u32[]{:S(2)}) collective-permute-start(bf16[256,256]{1,0:T(8,128)(2,1)S(1)} %product.2.refs_0_.prod_ref), channel_id=1, source_target_pairs={{0,0},{1,16},{2,32},{3,48},{4,64},{5,80},{6,96},{7,112},{8,128},{9... | collective-permute-start | bytes 393224 | tf_op jit(solution)/shard_map/ppermute | solution.py:38
  90.4 4.8 %collective-permute-done.9.refs_7_ = bf16[2,256,256]{2,1,0:T(8,128)(2,1)S(1)} collective-permute-done((bf16[2,256,256]{2,1,0:T(8,128)(2,1)S(1)}, bf16[2,256,256]{2,1,0:T(8,128)(2,1)S(1)}, u32[]{:S(2)}, u32[]{:S(2)}) %collective-permute-start.9) | collective-permute-done | bytes 262176 | tf_op jit(solution)/shard_map/ppermute | solution.py:34
  96.6 6.6 %collective-permute-start.29 = (bf16[256,256]{1,0:T(8,128)(2,1)S(1)}, bf16[256,256]{1,0:T(8,128)(2,1)S(1)}, u32[]{:S(2)}, u32[]{:S(2)}) collective-permute-start(bf16[256,256]{1,0:T(8,128)(2,1)S(1)} %get-tuple-element.19), channel_id=1, source_target_pairs={{128,0},{0,128},{129,1},{1,129},{130,2},{2,130},{131,3},{3,131},{1... | collective-permute-start | bytes 393224 | tf_op jit(solution)/shard_map/ppermute | solution.py:34
  103.2 3.1 %collective-permute-done.29.other_ref = bf16[256,256]{1,0:T(8,128)(2,1)S(1)} collective-permute-done((bf16[256,256]{1,0:T(8,128)(2,1)S(1)}, bf16[256,256]{1,0:T(8,128)(2,1)S(1)}, u32[]{:S(2)}, u32[]{:S(2)}) %collective-permute-start.29) | collective-permute-done | bytes 131104 | tf_op jit(solution)/shard_map/ppermute | solution.py:34
  106.4 3.6 %collective-permute-start.41 = (bf16[256,256]{1,0:T(8,128)(2,1)S(1)}, bf16[256,256]{1,0:T(8,128)(2,1)S(1)}, u32[]{:S(2)}, u32[]{:S(2)}) collective-permute-start(bf16[256,256]{1,0:T(8,128)(2,1)S(1)} %update.2.refs_0_.dens_ref), channel_id=1, source_target_pairs={{32,0},{64,32},{96,64},{0,96},{33,1},{65,33},{97,65},{1,97},{34,2}... | collective-permute-start | bytes 393224 | tf_op jit(solution)/shard_map/ppermute | solution.py:34
  112.5 6.2 %collective-permute-done.42.refs_2_ = bf16[256,256]{1,0:T(8,128)(2,1)S(1)} collective-permute-done((bf16[256,256]{1,0:T(8,128)(2,1)S(1)}, bf16[256,256]{1,0:T(8,128)(2,1)S(1)}, u32[]{:S(2)}, u32[]{:S(2)}) %collective-permute-start.42) | collective-permute-done | bytes 131104 | tf_op jit(solution)/shard_map/ppermute | solution.py:34
  125.1 4.3 %collective-permute-start.34 = (bf16[256,256]{1,0:T(8,128)(2,1)S(1)}, bf16[256,256]{1,0:T(8,128)(2,1)S(1)}, u32[]{:S(2)}, u32[]{:S(2)}) collective-permute-start(bf16[256,256]{1,0:T(8,128)(2,1)S(1)} %update.2.refs_0_.dens_ref), channel_id=1, source_target_pairs={{132,0},{128,4},{0,8},{4,12},{136,128},{140,132},{12,136},{8,140},... | collective-permute-start | bytes 393224 | tf_op jit(solution)/shard_map/ppermute | solution.py:115
  130.0 3.0 %collective-permute-start.32 = (bf16[256,256]{1,0:T(8,128)(2,1)S(1)}, bf16[256,256]{1,0:T(8,128)(2,1)S(1)}, u32[]{:S(2)}, u32[]{:S(2)}) collective-permute-start(bf16[256,256]{1,0:T(8,128)(2,1)S(1)} %update.2.refs_0_.dens_ref), channel_id=1, source_target_pairs={{128,0},{132,4},{4,8},{0,12},{140,128},{136,132},{8,136},{12,140},... | collective-permute-start | bytes 393224 | tf_op jit(solution)/shard_map/ppermute | solution.py:115
  134.0 3.0 %collective-permute-done.33.refs_0_ = bf16[256,256]{1,0:T(8,128)(2,1)S(1)} collective-permute-done((bf16[256,256]{1,0:T(8,128)(2,1)S(1)}, bf16[256,256]{1,0:T(8,128)(2,1)S(1)}, u32[]{:S(2)}, u32[]{:S(2)}) %collective-permute-start.33) | collective-permute-done | bytes 131104 | tf_op jit(solution)/shard_map/ppermute | solution.py:115
  144.1 3.0 %collective-permute-start.49 = (bf16[4,256,256]{2,1,0:T(8,128)(2,1)S(1)}, bf16[4,256,256]{2,1,0:T(8,128)(2,1)S(1)}, u32[]{:S(2)}, u32[]{:S(2)}) collective-permute-start(bf16[4,256,256]{2,1,0:T(8,128)(2,1)S(1)} %pack.19.refs_8_), channel_id=1, source_target_pairs={{16,0},{0,16},{17,1},{1,17},{18,2},{2,18},{19,3},{3,19},{20,4},{4,... | collective-permute-start | bytes 1572872 | tf_op jit(solution)/shard_map/ppermute | solution.py:34
  151.3 3.7 %collective-permute-done.36.refs_3_ = bf16[2,256,256]{2,1,0:T(8,128)(2,1)S(1)} collective-permute-done((bf16[2,256,256]{2,1,0:T(8,128)(2,1)S(1)}, bf16[2,256,256]{2,1,0:T(8,128)(2,1)S(1)}, u32[]{:S(2)}, u32[]{:S(2)}) %collective-permute-start.36) | collective-permute-done | bytes 262176 | tf_op jit(solution)/shard_map/ppermute | solution.py:34
  157.4 4.2 %collective-permute-done.40.refs_7_ = bf16[2,256,256]{2,1,0:T(8,128)(2,1)S(1)} collective-permute-done((bf16[2,256,256]{2,1,0:T(8,128)(2,1)S(1)}, bf16[2,256,256]{2,1,0:T(8,128)(2,1)S(1)}, u32[]{:S(2)}, u32[]{:S(2)}) %collective-permute-start.40) | collective-permute-done | bytes 262176 | tf_op jit(solution)/shard_map/ppermute | solution.py:34
  162.8 7.4 %collective-permute-start.50 = (bf16[256,256]{1,0:T(8,128)(2,1)S(1)}, bf16[256,256]{1,0:T(8,128)(2,1)S(1)}, u32[]{:S(2)}, u32[]{:S(2)}) collective-permute-start(bf16[256,256]{1,0:T(8,128)(2,1)S(1)} %get-tuple-element.23), channel_id=1, source_target_pairs={{128,0},{0,128},{129,1},{1,129},{130,2},{2,130},{131,3},{3,131},{1... | collective-permute-start | bytes 393224 | tf_op jit(solution)/shard_map/ppermute | solution.py:34
  (107 shorter events, 67.7 us)
Async XLA Ops:
  3.1 13.1 %collective-permute-start.20 = (bf16[256,256]{1,0:T(8,128)(2,1)S(1)}, bf16[256,256]{1,0:T(8,128)(2,1)S(1)}, u32[]{:S(2)}, u32[]{:S(2)}) collective-permute-start(bf16[256,256]{1,0:T(8,128)(2,1)S(1)} %get-tuple-element.14.refs_0_.dens_ref), channel_id=1, source_target_pairs={{32,0},{64,32},{96,64},{0,96},{33,1},{65,33},{97,65},{1,97},{34,2}... | collective-permute-start | bytes 393224 | tf_op jit(solution)/shard_map/ppermute | solution.py:34
  6.5 10.9 %collective-permute-start.21 = (bf16[256,256]{1,0:T(8,128)(2,1)S(1)}, bf16[256,256]{1,0:T(8,128)(2,1)S(1)}, u32[]{:S(2)}, u32[]{:S(2)}) collective-permute-start(bf16[256,256]{1,0:T(8,128)(2,1)S(1)} %get-tuple-element.14.refs_0_.dens_ref), channel_id=1, source_target_pairs={{96,0},{0,32},{32,64},{64,96},{97,1},{1,33},{33,65},{65,97},{98,2}... | collective-permute-start | bytes 393224 | tf_op jit(solution)/shard_map/ppermute | solution.py:34
  6.5 15.2 %collective-permute-start.22 = (bf16[256,256]{1,0:T(8,128)(2,1)S(1)}, bf16[256,256]{1,0:T(8,128)(2,1)S(1)}, u32[]{:S(2)}, u32[]{:S(2)}) collective-permute-start(bf16[256,256]{1,0:T(8,128)(2,1)S(1)} %get-tuple-element.14.refs_0_.dens_ref), channel_id=1, source_target_pairs={{64,0},{96,32},{0,64},{32,96},{65,1},{97,33},{1,65},{33,97},{66,2}... | collective-permute-start | bytes 393224 | tf_op jit(solution)/shard_map/ppermute | solution.py:34
  8.3 16.0 %collective-permute-start.10 = (bf16[256,256]{1,0:T(8,128)(2,1)S(1)}, bf16[256,256]{1,0:T(8,128)(2,1)S(1)}, u32[]{:S(2)}, u32[]{:S(2)}) collective-permute-start(bf16[256,256]{1,0:T(8,128)(2,1)S(1)} %get-tuple-element.15), channel_id=1, source_target_pairs={{0,0},{4,4},{132,8},{128,12},{12,128},{8,132},{136,136},{140,140},... | collective-permute-start | bytes 393224 | tf_op jit(solution)/shard_map/ppermute | solution.py:115
  8.9 19.2 %collective-permute-start.11 = (bf16[256,256]{1,0:T(8,128)(2,1)S(1)}, bf16[256,256]{1,0:T(8,128)(2,1)S(1)}, u32[]{:S(2)}, u32[]{:S(2)}) collective-permute-start(bf16[256,256]{1,0:T(8,128)(2,1)S(1)} %get-tuple-element.15), channel_id=1, source_target_pairs={{128,0},{132,4},{4,8},{0,12},{140,128},{136,132},{8,136},{12,140},... | collective-permute-start | bytes 393224 | tf_op jit(solution)/shard_map/ppermute | solution.py:115
  16.3 14.7 %collective-permute-start.12 = (bf16[256,256]{1,0:T(8,128)(2,1)S(1)}, bf16[256,256]{1,0:T(8,128)(2,1)S(1)}, u32[]{:S(2)}, u32[]{:S(2)}) collective-permute-start(bf16[256,256]{1,0:T(8,128)(2,1)S(1)} %get-tuple-element.15), channel_id=1, source_target_pairs={{4,0},{0,4},{128,8},{132,12},{8,128},{12,132},{140,136},{136,140},... | collective-permute-start | bytes 393224 | tf_op jit(solution)/shard_map/ppermute | solution.py:115
  17.4 13.5 %collective-permute-start.13 = (bf16[256,256]{1,0:T(8,128)(2,1)S(1)}, bf16[256,256]{1,0:T(8,128)(2,1)S(1)}, u32[]{:S(2)}, u32[]{:S(2)}) collective-permute-start(bf16[256,256]{1,0:T(8,128)(2,1)S(1)} %get-tuple-element.15), channel_id=1, source_target_pairs={{132,0},{128,4},{0,8},{4,12},{136,128},{140,132},{12,136},{8,140},... | collective-permute-start | bytes 393224 | tf_op jit(solution)/shard_map/ppermute | solution.py:115
  21.8 21.5 %collective-permute-start.23 = (bf16[4,256,256]{2,1,0:T(8,128)(2,1)S(1)}, bf16[4,256,256]{2,1,0:T(8,128)(2,1)S(1)}, u32[]{:S(2)}, u32[]{:S(2)}) collective-permute-start(bf16[4,256,256]{2,1,0:T(8,128)(2,1)S(1)} %pack.14.refs_8_), channel_id=1, source_target_pairs={{16,0},{0,16},{17,1},{1,17},{18,2},{2,18},{19,3},{3,19},{20,4},{4,... | collective-permute-start | bytes 1572872 | tf_op jit(solution)/shard_map/ppermute | solution.py:34
  34.3 11.4 %collective-permute-start.18 = (bf16[2,256,256]{2,1,0:T(8,128)(2,1)S(1)}, bf16[2,256,256]{2,1,0:T(8,128)(2,1)S(1)}, u32[]{:S(2)}, u32[]{:S(2)}) collective-permute-start(bf16[2,256,256]{2,1,0:T(8,128)(2,1)S(1)} %collective-permute-done.14.refs_2_), channel_id=1, source_target_pairs={{1,0},{2,1},{3,2},{0,3},{5,4},{6,5},{7,6},{4,7},{9,8},{10,9},{11,1... | collective-permute-start | bytes 786440 | tf_op jit(solution)/shard_map/ppermute | solution.py:34
  37.9 11.1 %collective-permute-start.19 = (bf16[2,256,256]{2,1,0:T(8,128)(2,1)S(1)}, bf16[2,256,256]{2,1,0:T(8,128)(2,1)S(1)}, u32[]{:S(2)}, u32[]{:S(2)}) collective-permute-start(bf16[2,256,256]{2,1,0:T(8,128)(2,1)S(1)} %collective-permute-done.17.refs_5_), channel_id=1, source_target_pairs={{3,0},{0,1},{1,2},{2,3},{7,4},{4,5},{5,6},{6,7},{11,8},{8,9},{9,10... | collective-permute-start | bytes 786440 | tf_op jit(solution)/shard_map/ppermute | solution.py:34
  50.2 15.3 %collective-permute-start.24 = (bf16[256,256]{1,0:T(8,128)(2,1)S(1)}, bf16[256,256]{1,0:T(8,128)(2,1)S(1)}, u32[]{:S(2)}, u32[]{:S(2)}) collective-permute-start(bf16[256,256]{1,0:T(8,128)(2,1)S(1)} %get-tuple-element.17), channel_id=1, source_target_pairs={{128,0},{0,128},{129,1},{1,129},{130,2},{2,130},{131,3},{3,131},{1... | collective-permute-start | bytes 393224 | tf_op jit(solution)/shard_map/ppermute | solution.py:34
  57.6 11.1 %collective-permute-start.2 = (bf16[256,256]{1,0:T(8,128)(2,1)S(1)}, bf16[256,256]{1,0:T(8,128)(2,1)S(1)}, u32[]{:S(2)}, u32[]{:S(2)}) collective-permute-start(bf16[256,256]{1,0:T(8,128)(2,1)S(1)} %get-tuple-element.14.refs_0_.dens_ref), channel_id=1, source_target_pairs={{4,0},{0,4},{128,8},{132,12},{8,128},{12,132},{140,136},{136,140},... | collective-permute-start | bytes 393224 | tf_op jit(solution)/shard_map/ppermute | solution.py:115
  57.6 12.6 %collective-permute-start.3 = (bf16[256,256]{1,0:T(8,128)(2,1)S(1)}, bf16[256,256]{1,0:T(8,128)(2,1)S(1)}, u32[]{:S(2)}, u32[]{:S(2)}) collective-permute-start(bf16[256,256]{1,0:T(8,128)(2,1)S(1)} %get-tuple-element.14.refs_0_.dens_ref), channel_id=1, source_target_pairs={{132,0},{128,4},{0,8},{4,12},{136,128},{140,132},{12,136},{8,140},... | collective-permute-start | bytes 393224 | tf_op jit(solution)/shard_map/ppermute | solution.py:115
  76.7 18.5 %collective-permute-start.28 = (bf16[4,256,256]{2,1,0:T(8,128)(2,1)S(1)}, bf16[4,256,256]{2,1,0:T(8,128)(2,1)S(1)}, u32[]{:S(2)}, u32[]{:S(2)}) collective-permute-start(bf16[4,256,256]{2,1,0:T(8,128)(2,1)S(1)} %pack.15.refs_8_), channel_id=1, source_target_pairs={{16,0},{0,16},{17,1},{1,17},{18,2},{2,18},{19,3},{3,19},{20,4},{4,... | collective-permute-start | bytes 1572872 | tf_op jit(solution)/shard_map/ppermute | solution.py:34
  80.9 14.3 %collective-permute-start.9 = (bf16[2,256,256]{2,1,0:T(8,128)(2,1)S(1)}, bf16[2,256,256]{2,1,0:T(8,128)(2,1)S(1)}, u32[]{:S(2)}, u32[]{:S(2)}) collective-permute-start(bf16[2,256,256]{2,1,0:T(8,128)(2,1)S(1)} %collective-permute-done.7.refs_5_), channel_id=1, source_target_pairs={{3,0},{0,1},{1,2},{2,3},{7,4},{4,5},{5,6},{6,7},{11,8},{8,9},{9,10... | collective-permute-start | bytes 786440 | tf_op jit(solution)/shard_map/ppermute | solution.py:34
  81.0 14.3 %collective-permute-start.8 = (bf16[2,256,256]{2,1,0:T(8,128)(2,1)S(1)}, bf16[2,256,256]{2,1,0:T(8,128)(2,1)S(1)}, u32[]{:S(2)}, u32[]{:S(2)}) collective-permute-start(bf16[2,256,256]{2,1,0:T(8,128)(2,1)S(1)} %collective-permute-done.4.refs_2_), channel_id=1, source_target_pairs={{1,0},{2,1},{3,2},{0,3},{5,4},{6,5},{7,6},{4,7},{9,8},{10,9},{11,1... | collective-permute-start | bytes 786440 | tf_op jit(solution)/shard_map/ppermute | solution.py:34
  87.3 15.9 %collective-permute-start.30 = (bf16[256,256]{1,0:T(8,128)(2,1)S(1)}, bf16[256,256]{1,0:T(8,128)(2,1)S(1)}, u32[]{:S(2)}, u32[]{:S(2)}) collective-permute-start(bf16[256,256]{1,0:T(8,128)(2,1)S(1)} %product.2.refs_0_.prod_ref), channel_id=1, source_target_pairs={{0,0},{1,16},{2,32},{3,48},{4,64},{5,80},{6,96},{7,112},{8,128},{9... | collective-permute-start | bytes 393224 | tf_op jit(solution)/shard_map/ppermute | solution.py:38
  125.1 12.0 %collective-permute-start.33 = (bf16[256,256]{1,0:T(8,128)(2,1)S(1)}, bf16[256,256]{1,0:T(8,128)(2,1)S(1)}, u32[]{:S(2)}, u32[]{:S(2)}) collective-permute-start(bf16[256,256]{1,0:T(8,128)(2,1)S(1)} %update.2.refs_0_.dens_ref), channel_id=1, source_target_pairs={{4,0},{0,4},{128,8},{132,12},{8,128},{12,132},{140,136},{136,140},... | collective-permute-start | bytes 393224 | tf_op jit(solution)/shard_map/ppermute | solution.py:115
  125.1 12.0 %collective-permute-start.34 = (bf16[256,256]{1,0:T(8,128)(2,1)S(1)}, bf16[256,256]{1,0:T(8,128)(2,1)S(1)}, u32[]{:S(2)}, u32[]{:S(2)}) collective-permute-start(bf16[256,256]{1,0:T(8,128)(2,1)S(1)} %update.2.refs_0_.dens_ref), channel_id=1, source_target_pairs={{132,0},{128,4},{0,8},{4,12},{136,128},{140,132},{12,136},{8,140},... | collective-permute-start | bytes 393224 | tf_op jit(solution)/shard_map/ppermute | solution.py:115
  144.1 17.5 %collective-permute-start.49 = (bf16[4,256,256]{2,1,0:T(8,128)(2,1)S(1)}, bf16[4,256,256]{2,1,0:T(8,128)(2,1)S(1)}, u32[]{:S(2)}, u32[]{:S(2)}) collective-permute-start(bf16[4,256,256]{2,1,0:T(8,128)(2,1)S(1)} %pack.19.refs_8_), channel_id=1, source_target_pairs={{16,0},{0,16},{17,1},{1,17},{18,2},{2,18},{19,3},{3,19},{20,4},{4,... | collective-permute-start | bytes 1572872 | tf_op jit(solution)/shard_map/ppermute | solution.py:34
  147.2 10.2 %collective-permute-start.37 = (bf16[2,256,256]{2,1,0:T(8,128)(2,1)S(1)}, bf16[2,256,256]{2,1,0:T(8,128)(2,1)S(1)}, u32[]{:S(2)}, u32[]{:S(2)}) collective-permute-start(bf16[2,256,256]{2,1,0:T(8,128)(2,1)S(1)} %pack.16.refs_0_), channel_id=1, source_target_pairs={{3,0},{0,1},{1,2},{2,3},{7,4},{4,5},{5,6},{6,7},{11,8},{8,9},{9,10... | collective-permute-start | bytes 786440 | tf_op jit(solution)/shard_map/ppermute | solution.py:34
  148.6 13.0 %collective-permute-start.40 = (bf16[2,256,256]{2,1,0:T(8,128)(2,1)S(1)}, bf16[2,256,256]{2,1,0:T(8,128)(2,1)S(1)}, u32[]{:S(2)}, u32[]{:S(2)}) collective-permute-start(bf16[2,256,256]{2,1,0:T(8,128)(2,1)S(1)} %collective-permute-done.38.refs_5_), channel_id=1, source_target_pairs={{3,0},{0,1},{1,2},{2,3},{7,4},{4,5},{5,6},{6,7},{11,8},{8,9},{9,10... | collective-permute-start | bytes 786440 | tf_op jit(solution)/shard_map/ppermute | solution.py:34
  148.6 12.9 %collective-permute-start.39 = (bf16[2,256,256]{2,1,0:T(8,128)(2,1)S(1)}, bf16[2,256,256]{2,1,0:T(8,128)(2,1)S(1)}, u32[]{:S(2)}, u32[]{:S(2)}) collective-permute-start(bf16[2,256,256]{2,1,0:T(8,128)(2,1)S(1)} %collective-permute-done.35.refs_2_), channel_id=1, source_target_pairs={{1,0},{2,1},{3,2},{0,3},{5,4},{6,5},{7,6},{4,7},{9,8},{10,9},{11,1... | collective-permute-start | bytes 786440 | tf_op jit(solution)/shard_map/ppermute | solution.py:34
  155.0 15.2 %collective-permute-start.51 = (bf16[256,256]{1,0:T(8,128)(2,1)S(1)}, bf16[256,256]{1,0:T(8,128)(2,1)S(1)}, u32[]{:S(2)}, u32[]{:S(2)}) collective-permute-start(bf16[256,256]{1,0:T(8,128)(2,1)S(1)} %product.3.refs_0_.prod_ref), channel_id=1, source_target_pairs={{0,0},{1,16},{2,32},{3,48},{4,64},{5,80},{6,96},{7,112},{8,128},{9... | collective-permute-start | bytes 393224 | tf_op jit(solution)/shard_map/ppermute | solution.py:38
  (31 other events, 232.9 us)

commit v2 on v1

v2 whole, which is shorter than its diff:
```python
import itertools

import jax
import jax.numpy as jnp
from jax import lax
from jax.experimental import pallas as pl
from jax.experimental.pallas import tpu as pltpu
from jax.sharding import Mesh
from jax.sharding import PartitionSpec as P

STEPS = 2
RATE = 0.1
ROW = ("zlo", "x", "core")
COL = ("zhi", "y")
SIZES = {"zlo": 2, "x": 4, "core": 2, "zhi": 4, "y": 4}
VMEM = pl.BlockSpec(memory_space=pltpu.VMEM)
SMEM = pl.BlockSpec(memory_space=pltpu.SMEM)
F32, BF16 = jnp.float32, jnp.bfloat16
BLOCK = jax.ShapeDtypeStruct((256, 256), BF16)
PAIR = jax.ShapeDtypeStruct((2, 256, 256), BF16)
BLOCK32 = jax.ShapeDtypeStruct((256, 256), F32)


def fetch(value, **offsets):
    axes = tuple(offsets)
    sizes = [SIZES[a] for a in axes]
    pairs = []
    for place in itertools.product(*[range(n) for n in sizes]):
        source = dest = 0
        for here, size, a in zip(place, sizes, axes):
            source = source * size + (here + offsets[a]) % size
            dest = dest * size + here
        pairs.append((source, dest))
    return lax.ppermute(value, axes, pairs)


def transposed(value):
    return lax.ppermute(value, ROW + COL, [(16 * i + j, 16 * j + i) for i in range(16) for j in range(16)])


def after(value, *others):
    return lax.optimization_barrier((value, *others))[0]


def call(kernel, outs, args, name, megabytes=4, flops=0):
    moved = sum(a.size * a.dtype.itemsize for a in args) + sum(o.size * o.dtype.itemsize for o in outs)
    return pl.pallas_call(
        kernel,
        out_shape=outs,
        in_specs=[SMEM if a.dtype == jnp.int32 else VMEM for a in args],
        out_specs=[VMEM] * len(outs),
        compiler_params=pltpu.CompilerParams(vmem_limit_bytes=megabytes << 20),
        cost_estimate=pl.CostEstimate(flops=flops, bytes_accessed=moved, transcendentals=0),
        name=name,
    )(*args)


def mask_kernel(keep_ref, in_ref, out_ref):
    out_ref[...] = (in_ref[...].astype(F32) * keep_ref[0, 0].astype(F32)).astype(BF16)


def pack_kernel(*refs):
    for n, ref in enumerate(refs[:-1]):
        refs[-1][n] = ref[...]


def pack(blocks):
    return call(pack_kernel, [jax.ShapeDtypeStruct((len(blocks), 256, 256), BF16)], blocks, "pack")[0]


def split_kernel(up_ref, down_ref, low_ref, high_ref):
    low_ref[...] = up_ref[:2]
    high_ref[...] = down_ref[2:]


def total(at_ref, refs):
    panel, (held_ref, swapped_ref) = refs[:-2], refs[-2:]
    acc = jnp.zeros((256, 256), F32)
    n = 0
    for ref in panel:
        for part in range(ref.shape[0]):
            place = at_ref[2 * n]
            block = jnp.where(at_ref[2 * n + 1] == 0, held_ref[place], swapped_ref[place])
            acc += jnp.dot(ref[part], block, preferred_element_type=F32)
            n += 1
    return acc


def product_kernel(keep_ref, at_ref, *refs):
    acc = total(at_ref, refs[:-1])
    refs[-1][...] = (acc * (keep_ref[0, 0].astype(F32) / 64.0)).astype(BF16)


def update_kernel(keep_ref, at_ref, prod_ref, turned_ref, dens_ref, *refs):
    refs, outs = refs[:7], refs[7:]
    triple = total(at_ref, refs) * (keep_ref[0, 0].astype(F32) / 64.0)
    gradient = prod_ref[...].astype(F32) + turned_ref[...].T.astype(F32) - 2.0 * triple
    outs[0][...] = (dens_ref[...].astype(F32) - RATE * gradient).astype(BF16)
    if len(outs) == 2:
        outs[1][...] = gradient


PANEL = ((0, (0, 1, 3, 2)), (1, (0, 1, 3, 2)), (3, (0, 1, 3, 2)), (2, (0, 1)), (2, (3, 2)))
FLOPS = 2 * 4096 * 256 * 256


def gather_z(block):
    return [block, fetch(block, zhi=1), fetch(block, zhi=3), fetch(block, zhi=2)]


def gather_y(held, *others):
    up, down = fetch(held, y=1), fetch(held, y=3)
    low, high = call(split_kernel, [PAIR, PAIR], [up, down], "split")
    return [held, up, down, fetch(after(low, *others), y=1), fetch(after(high, *others), y=3)]


def gather_x(block, early=(), late=()):
    pair = pack([block, fetch(block, zlo=1)])
    sent = after(pair, *early)
    held = join([pair, fetch(sent, x=1), fetch(sent, x=3), fetch(sent, x=2)])
    return [held, fetch(after(held, *late), core=1)]


def join_kernel(*refs):
    for n, ref in enumerate(refs[:-1]):
        refs[-1][2 * n : 2 * n + 2] = ref[...]


def join(pairs):
    return call(join_kernel, [jax.ShapeDtypeStruct((2 * len(pairs), 256, 256), BF16)], pairs, "join")[0]


def places():
    zlo, x, core, zhi, y = (lax.axis_index(a) for a in ROW + COL)
    rows = []
    for dy, dz in ((dy, dz) for dy, offsets in PANEL for dz in offsets):
        k = (zhi + dz) % 4 * 4 + (y + dy) % 4
        dx = (k // 2 % 4 - x) % 4
        step = jnp.where(dx == 0, 0, jnp.where(dx == 1, 1, jnp.where(dx == 3, 2, 3)))
        rows += [step * 2 + (k // 8 ^ zlo), (k % 2) ^ core]
    return jnp.stack(rows).astype(jnp.int32)


def local(hamiltonian, density, pattern):
    at = places()
    ham = call(mask_kernel, [BLOCK], [pattern, hamiltonian], "mask")[0]
    dens = call(mask_kernel, [BLOCK], [pattern, density], "mask")[0]
    ham_z = pack(gather_z(ham))
    ham_panel = gather_y(ham_z)
    dens = after(dens, ham_z)
    for step in range(STEPS):
        last = step == STEPS - 1
        dens_z = pack(gather_z(dens))
        dens_cols = gather_x(dens, (), (dens_z,) if step else (dens_z, *ham_panel[3:]))
        product = call(product_kernel, [BLOCK], [pattern, at, *ham_panel, *dens_cols], "product", 12, FLOPS)[0]
        turned = transposed(product)
        dens_panel = gather_y(dens_z, turned)
        prod_cols = gather_x(product, (), dens_panel[3:])
        outs = call(
            update_kernel,
            [BLOCK, BLOCK32] if last else [BLOCK],
            [pattern, at, product, turned, dens, *dens_panel, *prod_cols],
            "update",
            12,
            FLOPS,
        )
        dens = outs[0]
    return outs[1], dens


def solution(mesh):
    fine = Mesh(mesh.devices.reshape(2, 4, 2, 4, 4), ROW + COL)
    return jax.shard_map(
        local,
        mesh=fine,
        in_specs=(P(ROW, COL), P(ROW, COL), P(ROW, COL)),
        out_specs=(P(ROW, COL), P(ROW, COL)),
        check_vma=False,
    )
```

time: 175 us -> 155 us (0.89)
  starting transfers between devices: 107 us -> 76 us
  waiting for transfers between devices: 54.1 us -> 65.1 us
  Pallas kernels: 6.48 us -> 9.11 us
    ppermute x12 -> x0, starting transfers between devices: 29.3 us -> none  [start_z(): pieces.append(lax.ppermute(block, ('zlo', 'zhi'), pairs))]
    ppermute x38 -> x41, waiting for transfers between devices: 45.1 us -> 65 us  [fetch(): return lax.ppermute(value, axes, pairs)]
    ppermute x12 -> x0, waiting for transfers between devices: 9.04 us -> none  [start_z(): pieces.append(lax.ppermute(block, ('zlo', 'zhi'), pairs))]
    pallas_call x19 -> x20, Pallas kernels: 6.48 us -> 9.11 us  [call(): pl.pallas_call(kernel, out_shape=outs, in_specs=[SMEM if a.dtype == jnp.i...]
    ppermute x38 -> x41, starting transfers between devices: 72.3 us -> 71.8 us  [fetch(): return lax.ppermute(value, axes, pairs)]
  transfers between devices with their start and end apart: 52 -> 43, of which waited for: 18 -> 18; matrix products, arithmetic and copies ran while one was open for 0% -> 0% of each run, Pallas kernels for 2% -> 3%
where the time goes in v2:
time: 155 us; the launch traced here: 154 us
  starting transfers between devices  76 us (49%)
  waiting for transfers between devices  65.1 us (42%)
  Pallas kernels  9.11 us (6%)
  local copies, waits for them, and re-layouts  2.66 us (2%)
  between operations  1.59 us (1%)
    ppermute x41, starting transfers between devices, fetch(): return lax.ppermute(value, axes, pairs)  71.8 us
    ppermute x41, waiting for transfers between devices, fetch(): return lax.ppermute(value, axes, pairs)  65 us
    pallas_call x20, Pallas kernels, call(): pl.pallas_call(kernel, out_shape=outs, in_specs=[SMEM if a.dtype == jnp.i...  9.11 us
    ppermute x2, starting transfers between devices, transposed(): lax.ppermute(value, ROW + COL, [(16 * i + j, 16 * j + i) for i in range(1...  4.22 us
  transfers between devices with their start and end apart: 43, of which 18 were waited for; matrix products, arithmetic and copies ran while one was open for 0% of the time, Pallas kernels for 3%

profile of v2, /device:TPU:1, one launch (start us, length us, event | category | flops | bytes accessed | tf_op | source)
XLA Modules:
  0.0 154.4 jit_solution(17547224617021097174)
XLA Ops:
  2.2 7.8 %collective-permute-start.2 = (bf16[256,256]{1,0:T(8,128)(2,1)S(1)}, bf16[256,256]{1,0:T(8,128)(2,1)S(1)}, u32[]{:S(2)}, u32[]{:S(2)}) collective-permute-start(bf16[256,256]{1,0:T(8,128)(2,1)S(1)} %mask.2.refs_0_), channel_id=1, source_target_pairs={{8,0},{12,4},{0,8},{4,12},{9,1},{13,5},{1,9},{5,13},{10,2},{14,6},... | collective-permute-start | bytes 393224 | tf_op jit(solution)/shard_map/ppermute | solution.py:34
  11.2 2.4 %collective-permute-start = (bf16[256,256]{1,0:T(8,128)(2,1)S(1)}, bf16[256,256]{1,0:T(8,128)(2,1)S(1)}, u32[]{:S(2)}, u32[]{:S(2)}) collective-permute-start(bf16[256,256]{1,0:T(8,128)(2,1)S(1)} %mask.2.refs_0_), channel_id=1, source_target_pairs={{4,0},{8,4},{12,8},{0,12},{5,1},{9,5},{13,9},{1,13},{6,2},{10,6},{... | collective-permute-start | bytes 393224 | tf_op jit(solution)/shard_map/ppermute | solution.py:34
  13.6 5.3 %collective-permute-done.1.refs_2_ = bf16[256,256]{1,0:T(8,128)(2,1)S(1)} collective-permute-done((bf16[256,256]{1,0:T(8,128)(2,1)S(1)}, bf16[256,256]{1,0:T(8,128)(2,1)S(1)}, u32[]{:S(2)}, u32[]{:S(2)}) %collective-permute-start.1) | collective-permute-done | bytes 131104 | tf_op jit(solution)/shard_map/ppermute | solution.py:34
  19.0 4.0 %collective-permute-done.refs_1_ = bf16[256,256]{1,0:T(8,128)(2,1)S(1)} collective-permute-done((bf16[256,256]{1,0:T(8,128)(2,1)S(1)}, bf16[256,256]{1,0:T(8,128)(2,1)S(1)}, u32[]{:S(2)}, u32[]{:S(2)}) %collective-permute-start) | collective-permute-done | bytes 131104 | tf_op jit(solution)/shard_map/ppermute | solution.py:34
  26.1 4.2 %collective-permute-start.13 = (bf16[256,256]{1,0:T(8,128)(2,1)S(1)}, bf16[256,256]{1,0:T(8,128)(2,1)S(1)}, u32[]{:S(2)}, u32[]{:S(2)}) collective-permute-start(bf16[256,256]{1,0:T(8,128)(2,1)S(1)} %mask.3.refs_0_.dens_ref), channel_id=1, source_target_pairs={{8,0},{12,4},{0,8},{4,12},{9,1},{13,5},{1,9},{5,13},{10,2},{14,6},... | collective-permute-start | bytes 393224 | tf_op jit(solution)/shard_map/ppermute | solution.py:34
  33.8 3.5 %collective-permute-done.4.down_ref.refs_2_ = bf16[4,256,256]{2,1,0:T(8,128)(2,1)S(1)} collective-permute-done((bf16[4,256,256]{2,1,0:T(8,128)(2,1)S(1)}, bf16[4,256,256]{2,1,0:T(8,128)(2,1)S(1)}, u32[]{:S(2)}, u32[]{:S(2)}) %collective-permute-start.4) | collective-permute-done | bytes 524320 | tf_op jit(solution)/shard_map/ppermute | solution.py:34
  37.4 2.7 %collective-permute-start.10 = (bf16[2,256,256]{2,1,0:T(8,128)(2,1)S(1)}, bf16[2,256,256]{2,1,0:T(8,128)(2,1)S(1)}, u32[]{:S(2)}, u32[]{:S(2)}) collective-permute-start(bf16[2,256,256]{2,1,0:T(8,128)(2,1)S(1)} %pack.8.refs_0_), channel_id=1, source_target_pairs={{64,0},{96,32},{0,64},{32,96},{65,1},{97,33},{1,65},{33,97},{66,2}... | collective-permute-start | bytes 786440 | tf_op jit(solution)/shard_map/ppermute | solution.py:34
  40.5 2.4 %collective-permute-start.8 = (bf16[2,256,256]{2,1,0:T(8,128)(2,1)S(1)}, bf16[2,256,256]{2,1,0:T(8,128)(2,1)S(1)}, u32[]{:S(2)}, u32[]{:S(2)}) collective-permute-start(bf16[2,256,256]{2,1,0:T(8,128)(2,1)S(1)} %pack.8.refs_0_), channel_id=1, source_target_pairs={{32,0},{64,32},{96,64},{0,96},{33,1},{65,33},{97,65},{1,97},{34,2}... | collective-permute-start | bytes 786440 | tf_op jit(solution)/shard_map/ppermute | solution.py:34
  44.0 2.7 %collective-permute-start.5 = (bf16[2,256,256]{2,1,0:T(8,128)(2,1)S(1)}, bf16[2,256,256]{2,1,0:T(8,128)(2,1)S(1)}, u32[]{:S(2)}, u32[]{:S(2)}) collective-permute-start(bf16[2,256,256]{2,1,0:T(8,128)(2,1)S(1)} %get-tuple-element.19), channel_id=1, source_target_pairs={{1,0},{2,1},{3,2},{0,3},{5,4},{6,5},{7,6},{4,7},{9,8},{10,9},{11,1... | collective-permute-start | bytes 786440 | tf_op jit(solution)/shard_map/ppermute | solution.py:34
  46.7 5.7 %collective-permute-done.9.refs_2_ = bf16[2,256,256]{2,1,0:T(8,128)(2,1)S(1)} collective-permute-done((bf16[2,256,256]{2,1,0:T(8,128)(2,1)S(1)}, bf16[2,256,256]{2,1,0:T(8,128)(2,1)S(1)}, u32[]{:S(2)}, u32[]{:S(2)}) %collective-permute-start.9) | collective-permute-done | bytes 262176 | tf_op jit(solution)/shard_map/ppermute | solution.py:34
  54.6 2.7 %collective-permute-start.16 = (bf16[4,256,256]{2,1,0:T(8,128)(2,1)S(1)}, bf16[4,256,256]{2,1,0:T(8,128)(2,1)}, u32[]{:S(2)}, u32[]{:S(2)}) collective-permute-start(bf16[4,256,256]{2,1,0:T(8,128)(2,1)S(1)} %pack.9.refs_0_), channel_id=1, source_target_pairs={{1,0},{2,1},{3,2},{0,3},{5,4},{6,5},{7,6},{4,7},{9,8},{10,9},{11,1... | collective-permute-start | bytes 1572872 | tf_op jit(solution)/shard_map/ppermute | solution.py:34
  61.4 2.3 %collective-permute-start.15 = (bf16[256,256]{1,0:T(8,128)(2,1)S(1)}, bf16[256,256]{1,0:T(8,128)(2,1)S(1)}, u32[]{:S(2)}, u32[]{:S(2)}) collective-permute-start(bf16[256,256]{1,0:T(8,128)(2,1)S(1)} %product.2.refs_0_.prod_ref), channel_id=1, source_target_pairs={{0,0},{1,16},{2,32},{3,48},{4,64},{5,80},{6,96},{7,112},{8,128},{9... | collective-permute-start | bytes 393224 | tf_op jit(solution)/shard_map/ppermute | solution.py:38
  63.7 5.8 %collective-permute-done.17.down_ref.refs_2_ = bf16[4,256,256]{2,1,0:T(8,128)(2,1)} collective-permute-done((bf16[4,256,256]{2,1,0:T(8,128)(2,1)S(1)}, bf16[4,256,256]{2,1,0:T(8,128)(2,1)}, u32[]{:S(2)}, u32[]{:S(2)}) %collective-permute-start.17) | collective-permute-done | bytes 524320 | tf_op jit(solution)/shard_map/ppermute | solution.py:34
  74.9 2.3 %collective-permute-start.21 = (bf16[2,256,256]{2,1,0:T(8,128)(2,1)S(1)}, bf16[2,256,256]{2,1,0:T(8,128)(2,1)S(1)}, u32[]{:S(2)}, u32[]{:S(2)}) collective-permute-start(bf16[2,256,256]{2,1,0:T(8,128)(2,1)S(1)} %pack.10.refs_0_), channel_id=1, source_target_pairs={{32,0},{64,32},{96,64},{0,96},{33,1},{65,33},{97,65},{1,97},{34,2}... | collective-permute-start | bytes 786440 | tf_op jit(solution)/shard_map/ppermute | solution.py:34
  80.4 7.2 %collective-permute-done.22.refs_2_ = bf16[2,256,256]{2,1,0:T(8,128)(2,1)S(1)} collective-permute-done((bf16[2,256,256]{2,1,0:T(8,128)(2,1)S(1)}, bf16[2,256,256]{2,1,0:T(8,128)(2,1)S(1)}, u32[]{:S(2)}, u32[]{:S(2)}) %collective-permute-start.22) | collective-permute-done | bytes 262176 | tf_op jit(solution)/shard_map/ppermute | solution.py:34
  87.8 2.5 %collective-permute-start.24 = (bf16[8,256,256]{2,1,0:T(8,128)(2,1)S(1)}, bf16[8,256,256]{2,1,0:T(8,128)(2,1)S(1)}, u32[]{:S(2)}, u32[]{:S(2)}) collective-permute-start(bf16[8,256,256]{2,1,0:T(8,128)(2,1)S(1)} %join.5.refs_5_), channel_id=1, source_target_pairs={{16,0},{0,16},{17,1},{1,17},{18,2},{2,18},{19,3},{3,19},{20,4},{4,... | collective-permute-start | bytes 3145736 | tf_op jit(solution)/shard_map/ppermute | solution.py:34
  96.4 3.0 %collective-permute-done.25.refs_1_ = bf16[256,256]{1,0:T(8,128)(2,1)S(1)} collective-permute-done((bf16[256,256]{1,0:T(8,128)(2,1)S(1)}, bf16[256,256]{1,0:T(8,128)(2,1)S(1)}, u32[]{:S(2)}, u32[]{:S(2)}) %collective-permute-start.25) | collective-permute-done | bytes 131104 | tf_op jit(solution)/shard_map/ppermute | solution.py:34
  100.8 2.7 %collective-permute-start.26 = (bf16[2,256,256]{2,1,0:T(8,128)(2,1)S(1)}, bf16[2,256,256]{2,1,0:T(8,128)(2,1)S(1)}, u32[]{:S(2)}, u32[]{:S(2)}) collective-permute-start(bf16[2,256,256]{2,1,0:T(8,128)(2,1)S(1)} %pack.11.refs_0_), channel_id=1, source_target_pairs={{32,0},{64,32},{96,64},{0,96},{33,1},{65,33},{97,65},{1,97},{34,2}... | collective-permute-start | bytes 786440 | tf_op jit(solution)/shard_map/ppermute | solution.py:34
  104.0 5.6 %collective-permute-start.29 = (bf16[256,256]{1,0:T(8,128)(2,1)S(1)}, bf16[256,256]{1,0:T(8,128)(2,1)S(1)}, u32[]{:S(2)}, u32[]{:S(2)}) collective-permute-start(bf16[256,256]{1,0:T(8,128)(2,1)S(1)} %update.2.refs_0_.dens_ref), channel_id=1, source_target_pairs={{4,0},{8,4},{12,8},{0,12},{5,1},{9,5},{13,9},{1,13},{6,2},{10,6},{... | collective-permute-start | bytes 393224 | tf_op jit(solution)/shard_map/ppermute | solution.py:34
  109.7 3.6 %collective-permute-done.29.refs_1_ = bf16[256,256]{1,0:T(8,128)(2,1)S(1)} collective-permute-done((bf16[256,256]{1,0:T(8,128)(2,1)S(1)}, bf16[256,256]{1,0:T(8,128)(2,1)S(1)}, u32[]{:S(2)}, u32[]{:S(2)}) %collective-permute-start.29) | collective-permute-done | bytes 131104 | tf_op jit(solution)/shard_map/ppermute | solution.py:34
  113.4 3.9 %collective-permute-start.32 = (bf16[8,256,256]{2,1,0:T(8,128)(2,1)S(1)}, bf16[8,256,256]{2,1,0:T(8,128)(2,1)S(1)}, u32[]{:S(2)}, u32[]{:S(2)}) collective-permute-start(bf16[8,256,256]{2,1,0:T(8,128)(2,1)S(1)} %join.6.refs_5_), channel_id=1, source_target_pairs={{16,0},{0,16},{17,1},{1,17},{18,2},{2,18},{19,3},{3,19},{20,4},{4,... | collective-permute-start | bytes 3145736 | tf_op jit(solution)/shard_map/ppermute | solution.py:34
  125.0 7.0 %collective-permute-done.35.down_ref.refs_2_ = bf16[4,256,256]{2,1,0:T(8,128)(2,1)S(1)} collective-permute-done((bf16[4,256,256]{2,1,0:T(8,128)(2,1)S(1)}, bf16[4,256,256]{2,1,0:T(8,128)(2,1)S(1)}, u32[]{:S(2)}, u32[]{:S(2)}) %collective-permute-start.35) | collective-permute-done | bytes 524320 | tf_op jit(solution)/shard_map/ppermute | solution.py:34
  137.8 2.4 %collective-permute-start.36 = (bf16[2,256,256]{2,1,0:T(8,128)(2,1)S(1)}, bf16[2,256,256]{2,1,0:T(8,128)(2,1)S(1)}, u32[]{:S(2)}, u32[]{:S(2)}) collective-permute-start(bf16[2,256,256]{2,1,0:T(8,128)(2,1)S(1)} %get-tuple-element.30), channel_id=1, source_target_pairs={{1,0},{2,1},{3,2},{0,3},{5,4},{6,5},{7,6},{4,7},{9,8},{10,9},{11,1... | collective-permute-start | bytes 786440 | tf_op jit(solution)/shard_map/ppermute | solution.py:34
  142.2 7.2 %collective-permute-done.40.refs_2_ = bf16[2,256,256]{2,1,0:T(8,128)(2,1)S(1)} collective-permute-done((bf16[2,256,256]{2,1,0:T(8,128)(2,1)S(1)}, bf16[2,256,256]{2,1,0:T(8,128)(2,1)S(1)}, u32[]{:S(2)}, u32[]{:S(2)}) %collective-permute-start.40) | collective-permute-done | bytes 262176 | tf_op jit(solution)/shard_map/ppermute | solution.py:34
  (93 shorter events, 53.9 us)
Async XLA Ops:
  11.2 11.7 %collective-permute-start = (bf16[256,256]{1,0:T(8,128)(2,1)S(1)}, bf16[256,256]{1,0:T(8,128)(2,1)S(1)}, u32[]{:S(2)}, u32[]{:S(2)}) collective-permute-start(bf16[256,256]{1,0:T(8,128)(2,1)S(1)} %mask.2.refs_0_), channel_id=1, source_target_pairs={{4,0},{8,4},{12,8},{0,12},{5,1},{9,5},{13,9},{1,13},{6,2},{10,6},{... | collective-permute-start | bytes 393224 | tf_op jit(solution)/shard_map/ppermute | solution.py:34
  23.0 14.4 %collective-permute-start.4 = (bf16[4,256,256]{2,1,0:T(8,128)(2,1)S(1)}, bf16[4,256,256]{2,1,0:T(8,128)(2,1)S(1)}, u32[]{:S(2)}, u32[]{:S(2)}) collective-permute-start(bf16[4,256,256]{2,1,0:T(8,128)(2,1)S(1)} %pack.7.refs_0_), channel_id=1, source_target_pairs={{3,0},{0,1},{1,2},{2,3},{7,4},{4,5},{5,6},{6,7},{11,8},{8,9},{9,10... | collective-permute-start | bytes 1572872 | tf_op jit(solution)/shard_map/ppermute | solution.py:34
  24.4 15.7 %collective-permute-start.3 = (bf16[4,256,256]{2,1,0:T(8,128)(2,1)S(1)}, bf16[4,256,256]{2,1,0:T(8,128)(2,1)S(1)}, u32[]{:S(2)}, u32[]{:S(2)}) collective-permute-start(bf16[4,256,256]{2,1,0:T(8,128)(2,1)S(1)} %pack.7.refs_0_), channel_id=1, source_target_pairs={{1,0},{2,1},{3,2},{0,3},{5,4},{6,5},{7,6},{4,7},{9,8},{10,9},{11,1... | collective-permute-start | bytes 1572872 | tf_op jit(solution)/shard_map/ppermute | solution.py:34
  26.1 14.4 %collective-permute-start.13 = (bf16[256,256]{1,0:T(8,128)(2,1)S(1)}, bf16[256,256]{1,0:T(8,128)(2,1)S(1)}, u32[]{:S(2)}, u32[]{:S(2)}) collective-permute-start(bf16[256,256]{1,0:T(8,128)(2,1)S(1)} %mask.3.refs_0_.dens_ref), channel_id=1, source_target_pairs={{8,0},{12,4},{0,8},{4,12},{9,1},{13,5},{1,9},{5,13},{10,2},{14,6},... | collective-permute-start | bytes 393224 | tf_op jit(solution)/shard_map/ppermute | solution.py:34
  30.2 13.7 %collective-permute-start.12 = (bf16[256,256]{1,0:T(8,128)(2,1)S(1)}, bf16[256,256]{1,0:T(8,128)(2,1)S(1)}, u32[]{:S(2)}, u32[]{:S(2)}) collective-permute-start(bf16[256,256]{1,0:T(8,128)(2,1)S(1)} %mask.3.refs_0_.dens_ref), channel_id=1, source_target_pairs={{12,0},{0,4},{4,8},{8,12},{13,1},{1,5},{5,9},{9,13},{14,2},{2,6},{... | collective-permute-start | bytes 393224 | tf_op jit(solution)/shard_map/ppermute | solution.py:34
  31.6 12.4 %collective-permute-start.11 = (bf16[256,256]{1,0:T(8,128)(2,1)S(1)}, bf16[256,256]{1,0:T(8,128)(2,1)S(1)}, u32[]{:S(2)}, u32[]{:S(2)}) collective-permute-start(bf16[256,256]{1,0:T(8,128)(2,1)S(1)} %mask.3.refs_0_.dens_ref), channel_id=1, source_target_pairs={{4,0},{8,4},{12,8},{0,12},{5,1},{9,5},{13,9},{1,13},{6,2},{10,6},{... | collective-permute-start | bytes 393224 | tf_op jit(solution)/shard_map/ppermute | solution.py:34
  40.1 12.3 %collective-permute-start.9 = (bf16[2,256,256]{2,1,0:T(8,128)(2,1)S(1)}, bf16[2,256,256]{2,1,0:T(8,128)(2,1)S(1)}, u32[]{:S(2)}, u32[]{:S(2)}) collective-permute-start(bf16[2,256,256]{2,1,0:T(8,128)(2,1)S(1)} %pack.8.refs_0_), channel_id=1, source_target_pairs={{96,0},{0,32},{32,64},{64,96},{97,1},{1,33},{33,65},{65,97},{98,2}... | collective-permute-start | bytes 786440 | tf_op jit(solution)/shard_map/ppermute | solution.py:34
  40.5 11.9 %collective-permute-start.8 = (bf16[2,256,256]{2,1,0:T(8,128)(2,1)S(1)}, bf16[2,256,256]{2,1,0:T(8,128)(2,1)S(1)}, u32[]{:S(2)}, u32[]{:S(2)}) collective-permute-start(bf16[2,256,256]{2,1,0:T(8,128)(2,1)S(1)} %pack.8.refs_0_), channel_id=1, source_target_pairs={{32,0},{64,32},{96,64},{0,96},{33,1},{65,33},{97,65},{1,97},{34,2}... | collective-permute-start | bytes 786440 | tf_op jit(solution)/shard_map/ppermute | solution.py:34
  54.6 14.9 %collective-permute-start.17 = (bf16[4,256,256]{2,1,0:T(8,128)(2,1)S(1)}, bf16[4,256,256]{2,1,0:T(8,128)(2,1)}, u32[]{:S(2)}, u32[]{:S(2)}) collective-permute-start(bf16[4,256,256]{2,1,0:T(8,128)(2,1)S(1)} %pack.9.refs_0_), channel_id=1, source_target_pairs={{3,0},{0,1},{1,2},{2,3},{7,4},{4,5},{5,6},{6,7},{11,8},{8,9},{9,10... | collective-permute-start | bytes 1572872 | tf_op jit(solution)/shard_map/ppermute | solution.py:34
  54.6 16.4 %collective-permute-start.16 = (bf16[4,256,256]{2,1,0:T(8,128)(2,1)S(1)}, bf16[4,256,256]{2,1,0:T(8,128)(2,1)}, u32[]{:S(2)}, u32[]{:S(2)}) collective-permute-start(bf16[4,256,256]{2,1,0:T(8,128)(2,1)S(1)} %pack.9.refs_0_), channel_id=1, source_target_pairs={{1,0},{2,1},{3,2},{0,3},{5,4},{6,5},{7,6},{4,7},{9,8},{10,9},{11,1... | collective-permute-start | bytes 1572872 | tf_op jit(solution)/shard_map/ppermute | solution.py:34
  60.3 11.9 %collective-permute-start.20 = (bf16[256,256]{1,0:T(8,128)(2,1)S(1)}, bf16[256,256]{1,0:T(8,128)(2,1)S(1)}, u32[]{:S(2)}, u32[]{:S(2)}) collective-permute-start(bf16[256,256]{1,0:T(8,128)(2,1)S(1)} %product.2.refs_0_.prod_ref), channel_id=1, source_target_pairs={{128,0},{0,128},{129,1},{1,129},{130,2},{2,130},{131,3},{3,131},{1... | collective-permute-start | bytes 393224 | tf_op jit(solution)/shard_map/ppermute | solution.py:34
  61.4 15.9 %collective-permute-start.15 = (bf16[256,256]{1,0:T(8,128)(2,1)S(1)}, bf16[256,256]{1,0:T(8,128)(2,1)S(1)}, u32[]{:S(2)}, u32[]{:S(2)}) collective-permute-start(bf16[256,256]{1,0:T(8,128)(2,1)S(1)} %product.2.refs_0_.prod_ref), channel_id=1, source_target_pairs={{0,0},{1,16},{2,32},{3,48},{4,64},{5,80},{6,96},{7,112},{8,128},{9... | collective-permute-start | bytes 393224 | tf_op jit(solution)/shard_map/ppermute | solution.py:38
  73.6 14.1 %collective-permute-start.22 = (bf16[2,256,256]{2,1,0:T(8,128)(2,1)S(1)}, bf16[2,256,256]{2,1,0:T(8,128)(2,1)S(1)}, u32[]{:S(2)}, u32[]{:S(2)}) collective-permute-start(bf16[2,256,256]{2,1,0:T(8,128)(2,1)S(1)} %pack.10.refs_0_), channel_id=1, source_target_pairs={{96,0},{0,32},{32,64},{64,96},{97,1},{1,33},{33,65},{65,97},{98,2}... | collective-permute-start | bytes 786440 | tf_op jit(solution)/shard_map/ppermute | solution.py:34
  74.9 12.7 %collective-permute-start.21 = (bf16[2,256,256]{2,1,0:T(8,128)(2,1)S(1)}, bf16[2,256,256]{2,1,0:T(8,128)(2,1)S(1)}, u32[]{:S(2)}, u32[]{:S(2)}) collective-permute-start(bf16[2,256,256]{2,1,0:T(8,128)(2,1)S(1)} %pack.10.refs_0_), channel_id=1, source_target_pairs={{32,0},{64,32},{96,64},{0,96},{33,1},{65,33},{97,65},{1,97},{34,2}... | collective-permute-start | bytes 786440 | tf_op jit(solution)/shard_map/ppermute | solution.py:34
  99.4 13.9 %collective-permute-start.28 = (bf16[2,256,256]{2,1,0:T(8,128)(2,1)S(1)}, bf16[2,256,256]{2,1,0:T(8,128)(2,1)S(1)}, u32[]{:S(2)}, u32[]{:S(2)}) collective-permute-start(bf16[2,256,256]{2,1,0:T(8,128)(2,1)S(1)} %pack.11.refs_0_), channel_id=1, source_target_pairs={{64,0},{96,32},{0,64},{32,96},{65,1},{97,33},{1,65},{33,97},{66,2}... | collective-permute-start | bytes 786440 | tf_op jit(solution)/shard_map/ppermute | solution.py:34
  100.7 12.6 %collective-permute-start.27 = (bf16[2,256,256]{2,1,0:T(8,128)(2,1)S(1)}, bf16[2,256,256]{2,1,0:T(8,128)(2,1)S(1)}, u32[]{:S(2)}, u32[]{:S(2)}) collective-permute-start(bf16[2,256,256]{2,1,0:T(8,128)(2,1)S(1)} %pack.11.refs_0_), channel_id=1, source_target_pairs={{96,0},{0,32},{32,64},{64,96},{97,1},{1,33},{33,65},{65,97},{98,2}... | collective-permute-start | bytes 786440 | tf_op jit(solution)/shard_map/ppermute | solution.py:34
  100.8 12.6 %collective-permute-start.26 = (bf16[2,256,256]{2,1,0:T(8,128)(2,1)S(1)}, bf16[2,256,256]{2,1,0:T(8,128)(2,1)S(1)}, u32[]{:S(2)}, u32[]{:S(2)}) collective-permute-start(bf16[2,256,256]{2,1,0:T(8,128)(2,1)S(1)} %pack.11.refs_0_), channel_id=1, source_target_pairs={{32,0},{64,32},{96,64},{0,96},{33,1},{65,33},{97,65},{1,97},{34,2}... | collective-permute-start | bytes 786440 | tf_op jit(solution)/shard_map/ppermute | solution.py:34
  117.4 14.7 %collective-permute-start.35 = (bf16[4,256,256]{2,1,0:T(8,128)(2,1)S(1)}, bf16[4,256,256]{2,1,0:T(8,128)(2,1)S(1)}, u32[]{:S(2)}, u32[]{:S(2)}) collective-permute-start(bf16[4,256,256]{2,1,0:T(8,128)(2,1)S(1)} %pack.12.refs_0_), channel_id=1, source_target_pairs={{3,0},{0,1},{1,2},{2,3},{7,4},{4,5},{5,6},{6,7},{11,8},{8,9},{9,10... | collective-permute-start | bytes 1572872 | tf_op jit(solution)/shard_map/ppermute | solution.py:34
  117.8 16.0 %collective-permute-start.34 = (bf16[4,256,256]{2,1,0:T(8,128)(2,1)S(1)}, bf16[4,256,256]{2,1,0:T(8,128)(2,1)S(1)}, u32[]{:S(2)}, u32[]{:S(2)}) collective-permute-start(bf16[4,256,256]{2,1,0:T(8,128)(2,1)S(1)} %pack.12.refs_0_), channel_id=1, source_target_pairs={{1,0},{2,1},{3,2},{0,3},{5,4},{6,5},{7,6},{4,7},{9,8},{10,9},{11,1... | collective-permute-start | bytes 1572872 | tf_op jit(solution)/shard_map/ppermute | solution.py:34
  121.4 12.5 %collective-permute-start.38 = (bf16[256,256]{1,0:T(8,128)(2,1)S(1)}, bf16[256,256]{1,0:T(8,128)(2,1)S(1)}, u32[]{:S(2)}, u32[]{:S(2)}) collective-permute-start(bf16[256,256]{1,0:T(8,128)(2,1)S(1)} %product.3.refs_0_.prod_ref), channel_id=1, source_target_pairs={{128,0},{0,128},{129,1},{1,129},{130,2},{2,130},{131,3},{3,131},{1... | collective-permute-start | bytes 393224 | tf_op jit(solution)/shard_map/ppermute | solution.py:34
  123.1 14.7 %collective-permute-start.33 = (bf16[256,256]{1,0:T(8,128)(2,1)S(1)}, bf16[256,256]{1,0:T(8,128)(2,1)S(1)}, u32[]{:S(2)}, u32[]{:S(2)}) collective-permute-start(bf16[256,256]{1,0:T(8,128)(2,1)S(1)} %product.3.refs_0_.prod_ref), channel_id=1, source_target_pairs={{0,0},{1,16},{2,32},{3,48},{4,64},{5,80},{6,96},{7,112},{8,128},{9... | collective-permute-start | bytes 393224 | tf_op jit(solution)/shard_map/ppermute | solution.py:38
  134.2 15.2 %collective-permute-start.40 = (bf16[2,256,256]{2,1,0:T(8,128)(2,1)S(1)}, bf16[2,256,256]{2,1,0:T(8,128)(2,1)S(1)}, u32[]{:S(2)}, u32[]{:S(2)}) collective-permute-start(bf16[2,256,256]{2,1,0:T(8,128)(2,1)S(1)} %pack.13.refs_0_), channel_id=1, source_target_pairs={{96,0},{0,32},{32,64},{64,96},{97,1},{1,33},{33,65},{65,97},{98,2}... | collective-permute-start | bytes 786440 | tf_op jit(solution)/shard_map/ppermute | solution.py:34
  135.5 13.9 %collective-permute-start.39 = (bf16[2,256,256]{2,1,0:T(8,128)(2,1)S(1)}, bf16[2,256,256]{2,1,0:T(8,128)(2,1)S(1)}, u32[]{:S(2)}, u32[]{:S(2)}) collective-permute-start(bf16[2,256,256]{2,1,0:T(8,128)(2,1)S(1)} %pack.13.refs_0_), channel_id=1, source_target_pairs={{32,0},{64,32},{96,64},{0,96},{33,1},{65,33},{97,65},{1,97},{34,2}... | collective-permute-start | bytes 786440 | tf_op jit(solution)/shard_map/ppermute | solution.py:34
  137.8 11.6 %collective-permute-start.36 = (bf16[2,256,256]{2,1,0:T(8,128)(2,1)S(1)}, bf16[2,256,256]{2,1,0:T(8,128)(2,1)S(1)}, u32[]{:S(2)}, u32[]{:S(2)}) collective-permute-start(bf16[2,256,256]{2,1,0:T(8,128)(2,1)S(1)} %get-tuple-element.30), channel_id=1, source_target_pairs={{1,0},{2,1},{3,2},{0,3},{5,4},{6,5},{7,6},{4,7},{9,8},{10,9},{11,1... | collective-permute-start | bytes 786440 | tf_op jit(solution)/shard_map/ppermute | solution.py:34
  (24 other events, 178.7 us)

commit v3 on v2

--- a/solution.py
+++ b/solution.py
@@ -130,28 +130,38 @@
     return call(join_kernel, [jax.ShapeDtypeStruct((2 * len(pairs), 256, 256), BF16)], pairs, "join")[0]
 
 
+def places_kernel(out_ref):
+    zlo, x, core, zhi, y = (lax.axis_index(a) for a in ROW + COL)
+    n = 0
+    for dy, dz in ((dy, dz) for dy, offsets in PANEL for dz in offsets):
+        k = ((zhi + dz) & 3) * 4 + ((y + dy) & 3)
+        dx = ((k >> 1) - x) & 3
+        out_ref[n] = (dx ^ (dx >> 1)) * 2 + ((k >> 3) ^ zlo)
+        out_ref[n + 1] = (k & 1) ^ core
+        n += 2
+
+
 def places():
-    zlo, x, core, zhi, y = (lax.axis_index(a) for a in ROW + COL)
-    rows = []
-    for dy, dz in ((dy, dz) for dy, offsets in PANEL for dz in offsets):
-        k = (zhi + dz) % 4 * 4 + (y + dy) % 4
-        dx = (k // 2 % 4 - x) % 4
-        step = jnp.where(dx == 0, 0, jnp.where(dx == 1, 1, jnp.where(dx == 3, 2, 3)))
-        rows += [step * 2 + (k // 8 ^ zlo), (k % 2) ^ core]
-    return jnp.stack(rows).astype(jnp.int32)
+    return pl.pallas_call(
+        places_kernel,
+        out_shape=jax.ShapeDtypeStruct((32,), jnp.int32),
+        out_specs=SMEM,
+        compiler_params=pltpu.CompilerParams(vmem_limit_bytes=1 << 20),
+        name="places",
+    )()
 
 
 def local(hamiltonian, density, pattern):
     at = places()
     ham = call(mask_kernel, [BLOCK], [pattern, hamiltonian], "mask")[0]
     dens = call(mask_kernel, [BLOCK], [pattern, density], "mask")[0]
-    ham_z = pack(gather_z(ham))
+    around = gather_z(ham)
+    ham_z = pack([after(around[0], at), *around[1:]])
     ham_panel = gather_y(ham_z)
-    dens = after(dens, ham_z)
     for step in range(STEPS):
         last = step == STEPS - 1
-        dens_z = pack(gather_z(dens))
-        dens_cols = gather_x(dens, (), (dens_z,) if step else (dens_z, *ham_panel[3:]))
+        dens_z = pack(gather_z(dens if step else after(dens, ham_z)))
+        dens_cols = gather_x(dens, () if step else (ham_z,), (dens_z,) if step else (dens_z, *ham_panel[3:]))
         product = call(product_kernel, [BLOCK], [pattern, at, *ham_panel, *dens_cols], "product", 12, FLOPS)[0]
         turned = transposed(product)
         dens_panel = gather_y(dens_z, turned)

time: 155 us -> 151 us (0.974)
  Pallas kernels: 9.11 us -> 6.97 us
  local copies, waits for them, and re-layouts: 2.66 us -> 0.9 us
    pallas_call x20, Pallas kernels: 9.11 us -> 6.38 us  [call(): pl.pallas_call(kernel, out_shape=outs, in_specs=[SMEM if a.dtype == jnp.i...]
    ppermute x41, starting transfers between devices: 71.8 us -> 69.8 us  [fetch(): return lax.ppermute(value, axes, pairs)]
    unnamed x10 -> x4, local copies, waits for them, and re-layouts: 2.55 us -> 0.9 us
  transfers between devices with their start and end apart: 43 -> 43, of which waited for: 18 -> 19; matrix products, arithmetic and copies ran while one was open for 0% -> 0% of each run, Pallas kernels for 3% -> 2%
where the time goes in v3:
time: 151 us
  starting transfers between devices  74.9 us (50%)
  waiting for transfers between devices  66.5 us (44%)
  Pallas kernels  6.97 us (5%)
  between operations  1.55 us (1%)
    ppermute x41, starting transfers between devices, fetch(): return lax.ppermute(value, axes, pairs)  69.8 us
    ppermute x41, waiting for transfers between devices, fetch(): return lax.ppermute(value, axes, pairs)  66.5 us
    pallas_call x20, Pallas kernels, call(): pl.pallas_call(kernel, out_shape=outs, in_specs=[SMEM if a.dtype == jnp.i...  6.38 us
    ppermute x2, starting transfers between devices, transposed(): lax.ppermute(value, ROW + COL, [(16 * i + j, 16 * j + i) for i in range(1...  5.15 us
  transfers between devices with their start and end apart: 43, of which 19 were waited for; matrix products, arithmetic and copies ran while one was open for 0% of the time, Pallas kernels for 2%

profile of v3, /device:TPU:1, one launch (start us, length us, event | category | flops | bytes accessed | tf_op | source)
XLA Modules:
  0.0 150.9 jit_solution(16435936516938941443)
XLA Ops:
  2.2 7.8 %collective-permute-start.2 = (bf16[256,256]{1,0:T(8,128)(2,1)S(1)}, bf16[256,256]{1,0:T(8,128)(2,1)S(1)}, u32[]{:S(2)}, u32[]{:S(2)}) collective-permute-start(bf16[256,256]{1,0:T(8,128)(2,1)S(1)} %mask.2.refs_0_), channel_id=1, source_target_pairs={{8,0},{12,4},{0,8},{4,12},{9,1},{13,5},{1,9},{5,13},{10,2},{14,6},... | collective-permute-start | bytes 393224 | tf_op jit(solution)/shard_map/ppermute | solution.py:34
  11.2 2.4 %collective-permute-start = (bf16[256,256]{1,0:T(8,128)(2,1)S(1)}, bf16[256,256]{1,0:T(8,128)(2,1)S(1)}, u32[]{:S(2)}, u32[]{:S(2)}) collective-permute-start(bf16[256,256]{1,0:T(8,128)(2,1)S(1)} %mask.2.refs_0_), channel_id=1, source_target_pairs={{4,0},{8,4},{12,8},{0,12},{5,1},{9,5},{13,9},{1,13},{6,2},{10,6},{... | collective-permute-start | bytes 393224 | tf_op jit(solution)/shard_map/ppermute | solution.py:34
  14.2 4.7 %collective-permute-done.1.refs_2_ = bf16[256,256]{1,0:T(8,128)(2,1)S(1)} collective-permute-done((bf16[256,256]{1,0:T(8,128)(2,1)S(1)}, bf16[256,256]{1,0:T(8,128)(2,1)S(1)}, u32[]{:S(2)}, u32[]{:S(2)}) %collective-permute-start.1) | collective-permute-done | bytes 131104 | tf_op jit(solution)/shard_map/ppermute | solution.py:34
  19.0 4.0 %collective-permute-done.refs_1_ = bf16[256,256]{1,0:T(8,128)(2,1)S(1)} collective-permute-done((bf16[256,256]{1,0:T(8,128)(2,1)S(1)}, bf16[256,256]{1,0:T(8,128)(2,1)S(1)}, u32[]{:S(2)}, u32[]{:S(2)}) %collective-permute-start) | collective-permute-done | bytes 131104 | tf_op jit(solution)/shard_map/ppermute | solution.py:34
  26.0 4.2 %collective-permute-start.13 = (bf16[256,256]{1,0:T(8,128)(2,1)S(1)}, bf16[256,256]{1,0:T(8,128)(2,1)S(1)}, u32[]{:S(2)}, u32[]{:S(2)}) collective-permute-start(bf16[256,256]{1,0:T(8,128)(2,1)S(1)} %mask.3.refs_0_.dens_ref), channel_id=1, source_target_pairs={{8,0},{12,4},{0,8},{4,12},{9,1},{13,5},{1,9},{5,13},{10,2},{14,6},... | collective-permute-start | bytes 393224 | tf_op jit(solution)/shard_map/ppermute | solution.py:34
  33.8 3.5 %collective-permute-done.4.down_ref.refs_2_ = bf16[4,256,256]{2,1,0:T(8,128)(2,1)S(1)} collective-permute-done((bf16[4,256,256]{2,1,0:T(8,128)(2,1)S(1)}, bf16[4,256,256]{2,1,0:T(8,128)(2,1)S(1)}, u32[]{:S(2)}, u32[]{:S(2)}) %collective-permute-start.4) | collective-permute-done | bytes 524320 | tf_op jit(solution)/shard_map/ppermute | solution.py:34
  37.4 2.7 %collective-permute-start.10 = (bf16[2,256,256]{2,1,0:T(8,128)(2,1)S(1)}, bf16[2,256,256]{2,1,0:T(8,128)(2,1)S(1)}, u32[]{:S(2)}, u32[]{:S(2)}) collective-permute-start(bf16[2,256,256]{2,1,0:T(8,128)(2,1)S(1)} %pack.8.refs_0_), channel_id=1, source_target_pairs={{64,0},{96,32},{0,64},{32,96},{65,1},{97,33},{1,65},{33,97},{66,2}... | collective-permute-start | bytes 786440 | tf_op jit(solution)/shard_map/ppermute | solution.py:34
  40.5 2.4 %collective-permute-start.8 = (bf16[2,256,256]{2,1,0:T(8,128)(2,1)S(1)}, bf16[2,256,256]{2,1,0:T(8,128)(2,1)S(1)}, u32[]{:S(2)}, u32[]{:S(2)}) collective-permute-start(bf16[2,256,256]{2,1,0:T(8,128)(2,1)S(1)} %pack.8.refs_0_), channel_id=1, source_target_pairs={{32,0},{64,32},{96,64},{0,96},{33,1},{65,33},{97,65},{1,97},{34,2}... | collective-permute-start | bytes 786440 | tf_op jit(solution)/shard_map/ppermute | solution.py:34
  43.9 2.7 %collective-permute-start.5 = (bf16[2,256,256]{2,1,0:T(8,128)(2,1)S(1)}, bf16[2,256,256]{2,1,0:T(8,128)(2,1)S(1)}, u32[]{:S(2)}, u32[]{:S(2)}) collective-permute-start(bf16[2,256,256]{2,1,0:T(8,128)(2,1)S(1)} %get-tuple-element.22), channel_id=1, source_target_pairs={{1,0},{2,1},{3,2},{0,3},{5,4},{6,5},{7,6},{4,7},{9,8},{10,9},{11,1... | collective-permute-start | bytes 786440 | tf_op jit(solution)/shard_map/ppermute | solution.py:34
  46.7 5.7 %collective-permute-done.9.refs_2_ = bf16[2,256,256]{2,1,0:T(8,128)(2,1)S(1)} collective-permute-done((bf16[2,256,256]{2,1,0:T(8,128)(2,1)S(1)}, bf16[2,256,256]{2,1,0:T(8,128)(2,1)S(1)}, u32[]{:S(2)}, u32[]{:S(2)}) %collective-permute-start.9) | collective-permute-done | bytes 262176 | tf_op jit(solution)/shard_map/ppermute | solution.py:34
  53.9 2.7 %collective-permute-start.16 = (bf16[4,256,256]{2,1,0:T(8,128)(2,1)S(1)}, bf16[4,256,256]{2,1,0:T(8,128)(2,1)S(1)}, u32[]{:S(2)}, u32[]{:S(2)}) collective-permute-start(bf16[4,256,256]{2,1,0:T(8,128)(2,1)S(1)} %pack.9.refs_0_), channel_id=1, source_target_pairs={{1,0},{2,1},{3,2},{0,3},{5,4},{6,5},{7,6},{4,7},{9,8},{10,9},{11,1... | collective-permute-start | bytes 1572872 | tf_op jit(solution)/shard_map/ppermute | solution.py:34
  61.2 7.5 %collective-permute-done.17.down_ref.refs_2_ = bf16[4,256,256]{2,1,0:T(8,128)(2,1)S(1)} collective-permute-done((bf16[4,256,256]{2,1,0:T(8,128)(2,1)S(1)}, bf16[4,256,256]{2,1,0:T(8,128)(2,1)S(1)}, u32[]{:S(2)}, u32[]{:S(2)}) %collective-permute-start.17) | collective-permute-done | bytes 524320 | tf_op jit(solution)/shard_map/ppermute | solution.py:34
  75.2 3.3 %collective-permute-start.18 = (bf16[2,256,256]{2,1,0:T(8,128)(2,1)S(1)}, bf16[2,256,256]{2,1,0:T(8,128)(2,1)S(1)}, u32[]{:S(2)}, u32[]{:S(2)}) collective-permute-start(bf16[2,256,256]{2,1,0:T(8,128)(2,1)S(1)} %get-tuple-element.28), channel_id=1, source_target_pairs={{1,0},{2,1},{3,2},{0,3},{5,4},{6,5},{7,6},{4,7},{9,8},{10,9},{11,1... | collective-permute-start | bytes 786440 | tf_op jit(solution)/shard_map/ppermute | solution.py:34
  78.8 7.0 %collective-permute-done.22.refs_2_ = bf16[2,256,256]{2,1,0:T(8,128)(2,1)S(1)} collective-permute-done((bf16[2,256,256]{2,1,0:T(8,128)(2,1)S(1)}, bf16[2,256,256]{2,1,0:T(8,128)(2,1)S(1)}, u32[]{:S(2)}, u32[]{:S(2)}) %collective-permute-start.22) | collective-permute-done | bytes 262176 | tf_op jit(solution)/shard_map/ppermute | solution.py:34
  85.9 3.3 %collective-permute-start.24 = (bf16[8,256,256]{2,1,0:T(8,128)(2,1)S(1)}, bf16[8,256,256]{2,1,0:T(8,128)(2,1)S(1)}, u32[]{:S(2)}, u32[]{:S(2)}) collective-permute-start(bf16[8,256,256]{2,1,0:T(8,128)(2,1)S(1)} %join.5.refs_5_), channel_id=1, source_target_pairs={{16,0},{0,16},{17,1},{1,17},{18,2},{2,18},{19,3},{3,19},{20,4},{4,... | collective-permute-start | bytes 3145736 | tf_op jit(solution)/shard_map/ppermute | solution.py:34
  95.2 2.4 %collective-permute-done.25.refs_1_ = bf16[256,256]{1,0:T(8,128)(2,1)S(1)} collective-permute-done((bf16[256,256]{1,0:T(8,128)(2,1)S(1)}, bf16[256,256]{1,0:T(8,128)(2,1)S(1)}, u32[]{:S(2)}, u32[]{:S(2)}) %collective-permute-start.25) | collective-permute-done | bytes 131104 | tf_op jit(solution)/shard_map/ppermute | solution.py:34
  98.0 2.7 %collective-permute-start.26 = (bf16[2,256,256]{2,1,0:T(8,128)(2,1)S(1)}, bf16[2,256,256]{2,1,0:T(8,128)(2,1)S(1)}, u32[]{:S(2)}, u32[]{:S(2)}) collective-permute-start(bf16[2,256,256]{2,1,0:T(8,128)(2,1)S(1)} %pack.11.refs_0_), channel_id=1, source_target_pairs={{32,0},{64,32},{96,64},{0,96},{33,1},{65,33},{97,65},{1,97},{34,2}... | collective-permute-start | bytes 786440 | tf_op jit(solution)/shard_map/ppermute | solution.py:34
  101.9 4.9 %collective-permute-start.29 = (bf16[256,256]{1,0:T(8,128)(2,1)S(1)}, bf16[256,256]{1,0:T(8,128)(2,1)S(1)}, u32[]{:S(2)}, u32[]{:S(2)}) collective-permute-start(bf16[256,256]{1,0:T(8,128)(2,1)S(1)} %update.2.refs_0_.dens_ref), channel_id=1, source_target_pairs={{4,0},{8,4},{12,8},{0,12},{5,1},{9,5},{13,9},{1,13},{6,2},{10,6},{... | collective-permute-start | bytes 393224 | tf_op jit(solution)/shard_map/ppermute | solution.py:34
  107.0 5.1 %collective-permute-done.29.refs_1_ = bf16[256,256]{1,0:T(8,128)(2,1)S(1)} collective-permute-done((bf16[256,256]{1,0:T(8,128)(2,1)S(1)}, bf16[256,256]{1,0:T(8,128)(2,1)S(1)}, u32[]{:S(2)}, u32[]{:S(2)}) %collective-permute-start.29) | collective-permute-done | bytes 131104 | tf_op jit(solution)/shard_map/ppermute | solution.py:34
  113.7 2.7 %collective-permute-start.34 = (bf16[4,256,256]{2,1,0:T(8,128)(2,1)S(1)}, bf16[4,256,256]{2,1,0:T(8,128)(2,1)S(1)}, u32[]{:S(2)}, u32[]{:S(2)}) collective-permute-start(bf16[4,256,256]{2,1,0:T(8,128)(2,1)S(1)} %pack.12.refs_0_), channel_id=1, source_target_pairs={{1,0},{2,1},{3,2},{0,3},{5,4},{6,5},{7,6},{4,7},{9,8},{10,9},{11,1... | collective-permute-start | bytes 1572872 | tf_op jit(solution)/shard_map/ppermute | solution.py:34
  117.8 2.9 %collective-permute-start.33 = (bf16[256,256]{1,0:T(8,128)(2,1)S(1)}, bf16[256,256]{1,0:T(8,128)(2,1)S(1)}, u32[]{:S(2)}, u32[]{:S(2)}) collective-permute-start(bf16[256,256]{1,0:T(8,128)(2,1)S(1)} %product.3.refs_0_.prod_ref), channel_id=1, source_target_pairs={{0,0},{1,16},{2,32},{3,48},{4,64},{5,80},{6,96},{7,112},{8,128},{9... | collective-permute-start | bytes 393224 | tf_op jit(solution)/shard_map/ppermute | solution.py:38
  120.7 7.7 %collective-permute-done.35.down_ref.refs_2_ = bf16[4,256,256]{2,1,0:T(8,128)(2,1)S(1)} collective-permute-done((bf16[4,256,256]{2,1,0:T(8,128)(2,1)S(1)}, bf16[4,256,256]{2,1,0:T(8,128)(2,1)S(1)}, u32[]{:S(2)}, u32[]{:S(2)}) %collective-permute-start.35) | collective-permute-done | bytes 524320 | tf_op jit(solution)/shard_map/ppermute | solution.py:34
  133.8 2.9 %collective-permute-start.36 = (bf16[2,256,256]{2,1,0:T(8,128)(2,1)S(1)}, bf16[2,256,256]{2,1,0:T(8,128)(2,1)S(1)}, u32[]{:S(2)}, u32[]{:S(2)}) collective-permute-start(bf16[2,256,256]{2,1,0:T(8,128)(2,1)S(1)} %get-tuple-element.34), channel_id=1, source_target_pairs={{1,0},{2,1},{3,2},{0,3},{5,4},{6,5},{7,6},{4,7},{9,8},{10,9},{11,1... | collective-permute-start | bytes 786440 | tf_op jit(solution)/shard_map/ppermute | solution.py:34
  138.4 7.2 %collective-permute-done.40.refs_2_ = bf16[2,256,256]{2,1,0:T(8,128)(2,1)S(1)} collective-permute-done((bf16[2,256,256]{2,1,0:T(8,128)(2,1)S(1)}, bf16[2,256,256]{2,1,0:T(8,128)(2,1)S(1)}, u32[]{:S(2)}, u32[]{:S(2)}) %collective-permute-start.40) | collective-permute-done | bytes 262176 | tf_op jit(solution)/shard_map/ppermute | solution.py:34
  (87 shorter events, 47.2 us)
Async XLA Ops:
  2.2 12.0 %collective-permute-start.2 = (bf16[256,256]{1,0:T(8,128)(2,1)S(1)}, bf16[256,256]{1,0:T(8,128)(2,1)S(1)}, u32[]{:S(2)}, u32[]{:S(2)}) collective-permute-start(bf16[256,256]{1,0:T(8,128)(2,1)S(1)} %mask.2.refs_0_), channel_id=1, source_target_pairs={{8,0},{12,4},{0,8},{4,12},{9,1},{13,5},{1,9},{5,13},{10,2},{14,6},... | collective-permute-start | bytes 393224 | tf_op jit(solution)/shard_map/ppermute | solution.py:34
  23.0 14.4 %collective-permute-start.4 = (bf16[4,256,256]{2,1,0:T(8,128)(2,1)S(1)}, bf16[4,256,256]{2,1,0:T(8,128)(2,1)S(1)}, u32[]{:S(2)}, u32[]{:S(2)}) collective-permute-start(bf16[4,256,256]{2,1,0:T(8,128)(2,1)S(1)} %pack.7.refs_0_), channel_id=1, source_target_pairs={{3,0},{0,1},{1,2},{2,3},{7,4},{4,5},{5,6},{6,7},{11,8},{8,9},{9,10... | collective-permute-start | bytes 1572872 | tf_op jit(solution)/shard_map/ppermute | solution.py:34
  24.4 15.7 %collective-permute-start.3 = (bf16[4,256,256]{2,1,0:T(8,128)(2,1)S(1)}, bf16[4,256,256]{2,1,0:T(8,128)(2,1)S(1)}, u32[]{:S(2)}, u32[]{:S(2)}) collective-permute-start(bf16[4,256,256]{2,1,0:T(8,128)(2,1)S(1)} %pack.7.refs_0_), channel_id=1, source_target_pairs={{1,0},{2,1},{3,2},{0,3},{5,4},{6,5},{7,6},{4,7},{9,8},{10,9},{11,1... | collective-permute-start | bytes 1572872 | tf_op jit(solution)/shard_map/ppermute | solution.py:34
  26.0 14.4 %collective-permute-start.13 = (bf16[256,256]{1,0:T(8,128)(2,1)S(1)}, bf16[256,256]{1,0:T(8,128)(2,1)S(1)}, u32[]{:S(2)}, u32[]{:S(2)}) collective-permute-start(bf16[256,256]{1,0:T(8,128)(2,1)S(1)} %mask.3.refs_0_.dens_ref), channel_id=1, source_target_pairs={{8,0},{12,4},{0,8},{4,12},{9,1},{13,5},{1,9},{5,13},{10,2},{14,6},... | collective-permute-start | bytes 393224 | tf_op jit(solution)/shard_map/ppermute | solution.py:34
  30.2 13.7 %collective-permute-start.12 = (bf16[256,256]{1,0:T(8,128)(2,1)S(1)}, bf16[256,256]{1,0:T(8,128)(2,1)S(1)}, u32[]{:S(2)}, u32[]{:S(2)}) collective-permute-start(bf16[256,256]{1,0:T(8,128)(2,1)S(1)} %mask.3.refs_0_.dens_ref), channel_id=1, source_target_pairs={{12,0},{0,4},{4,8},{8,12},{13,1},{1,5},{5,9},{9,13},{14,2},{2,6},{... | collective-permute-start | bytes 393224 | tf_op jit(solution)/shard_map/ppermute | solution.py:34
  31.6 12.4 %collective-permute-start.11 = (bf16[256,256]{1,0:T(8,128)(2,1)S(1)}, bf16[256,256]{1,0:T(8,128)(2,1)S(1)}, u32[]{:S(2)}, u32[]{:S(2)}) collective-permute-start(bf16[256,256]{1,0:T(8,128)(2,1)S(1)} %mask.3.refs_0_.dens_ref), channel_id=1, source_target_pairs={{4,0},{8,4},{12,8},{0,12},{5,1},{9,5},{13,9},{1,13},{6,2},{10,6},{... | collective-permute-start | bytes 393224 | tf_op jit(solution)/shard_map/ppermute | solution.py:34
  40.1 12.3 %collective-permute-start.9 = (bf16[2,256,256]{2,1,0:T(8,128)(2,1)S(1)}, bf16[2,256,256]{2,1,0:T(8,128)(2,1)S(1)}, u32[]{:S(2)}, u32[]{:S(2)}) collective-permute-start(bf16[2,256,256]{2,1,0:T(8,128)(2,1)S(1)} %pack.8.refs_0_), channel_id=1, source_target_pairs={{96,0},{0,32},{32,64},{64,96},{97,1},{1,33},{33,65},{65,97},{98,2}... | collective-permute-start | bytes 786440 | tf_op jit(solution)/shard_map/ppermute | solution.py:34
  40.5 11.9 %collective-permute-start.8 = (bf16[2,256,256]{2,1,0:T(8,128)(2,1)S(1)}, bf16[2,256,256]{2,1,0:T(8,128)(2,1)S(1)}, u32[]{:S(2)}, u32[]{:S(2)}) collective-permute-start(bf16[2,256,256]{2,1,0:T(8,128)(2,1)S(1)} %pack.8.refs_0_), channel_id=1, source_target_pairs={{32,0},{64,32},{96,64},{0,96},{33,1},{65,33},{97,65},{1,97},{34,2}... | collective-permute-start | bytes 786440 | tf_op jit(solution)/shard_map/ppermute | solution.py:34
  53.9 14.8 %collective-permute-start.17 = (bf16[4,256,256]{2,1,0:T(8,128)(2,1)S(1)}, bf16[4,256,256]{2,1,0:T(8,128)(2,1)S(1)}, u32[]{:S(2)}, u32[]{:S(2)}) collective-permute-start(bf16[4,256,256]{2,1,0:T(8,128)(2,1)S(1)} %pack.9.refs_0_), channel_id=1, source_target_pairs={{3,0},{0,1},{1,2},{2,3},{7,4},{4,5},{5,6},{6,7},{11,8},{8,9},{9,10... | collective-permute-start | bytes 1572872 | tf_op jit(solution)/shard_map/ppermute | solution.py:34
  53.9 16.5 %collective-permute-start.16 = (bf16[4,256,256]{2,1,0:T(8,128)(2,1)S(1)}, bf16[4,256,256]{2,1,0:T(8,128)(2,1)S(1)}, u32[]{:S(2)}, u32[]{:S(2)}) collective-permute-start(bf16[4,256,256]{2,1,0:T(8,128)(2,1)S(1)} %pack.9.refs_0_), channel_id=1, source_target_pairs={{1,0},{2,1},{3,2},{0,3},{5,4},{6,5},{7,6},{4,7},{9,8},{10,9},{11,1... | collective-permute-start | bytes 1572872 | tf_op jit(solution)/shard_map/ppermute | solution.py:34
  57.8 12.6 %collective-permute-start.20 = (bf16[256,256]{1,0:T(8,128)(2,1)S(1)}, bf16[256,256]{1,0:T(8,128)(2,1)S(1)}, u32[]{:S(2)}, u32[]{:S(2)}) collective-permute-start(bf16[256,256]{1,0:T(8,128)(2,1)S(1)} %product.2.refs_0_.prod_ref), channel_id=1, source_target_pairs={{128,0},{0,128},{129,1},{1,129},{130,2},{2,130},{131,3},{3,131},{1... | collective-permute-start | bytes 393224 | tf_op jit(solution)/shard_map/ppermute | solution.py:34
  58.9 16.4 %collective-permute-start.15 = (bf16[256,256]{1,0:T(8,128)(2,1)S(1)}, bf16[256,256]{1,0:T(8,128)(2,1)S(1)}, u32[]{:S(2)}, u32[]{:S(2)}) collective-permute-start(bf16[256,256]{1,0:T(8,128)(2,1)S(1)} %product.2.refs_0_.prod_ref), channel_id=1, source_target_pairs={{0,0},{1,16},{2,32},{3,48},{4,64},{5,80},{6,96},{7,112},{8,128},{9... | collective-permute-start | bytes 393224 | tf_op jit(solution)/shard_map/ppermute | solution.py:38
  72.2 13.6 %collective-permute-start.22 = (bf16[2,256,256]{2,1,0:T(8,128)(2,1)S(1)}, bf16[2,256,256]{2,1,0:T(8,128)(2,1)S(1)}, u32[]{:S(2)}, u32[]{:S(2)}) collective-permute-start(bf16[2,256,256]{2,1,0:T(8,128)(2,1)S(1)} %pack.10.refs_0_), channel_id=1, source_target_pairs={{96,0},{0,32},{32,64},{64,96},{97,1},{1,33},{33,65},{65,97},{98,2}... | collective-permute-start | bytes 786440 | tf_op jit(solution)/shard_map/ppermute | solution.py:34
  72.9 12.9 %collective-permute-start.21 = (bf16[2,256,256]{2,1,0:T(8,128)(2,1)S(1)}, bf16[2,256,256]{2,1,0:T(8,128)(2,1)S(1)}, u32[]{:S(2)}, u32[]{:S(2)}) collective-permute-start(bf16[2,256,256]{2,1,0:T(8,128)(2,1)S(1)} %pack.10.refs_0_), channel_id=1, source_target_pairs={{32,0},{64,32},{96,64},{0,96},{33,1},{65,33},{97,65},{1,97},{34,2}... | collective-permute-start | bytes 786440 | tf_op jit(solution)/shard_map/ppermute | solution.py:34
  97.6 14.6 %collective-permute-start.28 = (bf16[2,256,256]{2,1,0:T(8,128)(2,1)S(1)}, bf16[2,256,256]{2,1,0:T(8,128)(2,1)S(1)}, u32[]{:S(2)}, u32[]{:S(2)}) collective-permute-start(bf16[2,256,256]{2,1,0:T(8,128)(2,1)S(1)} %pack.11.refs_0_), channel_id=1, source_target_pairs={{64,0},{96,32},{0,64},{32,96},{65,1},{97,33},{1,65},{33,97},{66,2}... | collective-permute-start | bytes 786440 | tf_op jit(solution)/shard_map/ppermute | solution.py:34
  98.0 14.6 %collective-permute-start.27 = (bf16[2,256,256]{2,1,0:T(8,128)(2,1)S(1)}, bf16[2,256,256]{2,1,0:T(8,128)(2,1)S(1)}, u32[]{:S(2)}, u32[]{:S(2)}) collective-permute-start(bf16[2,256,256]{2,1,0:T(8,128)(2,1)S(1)} %pack.11.refs_0_), channel_id=1, source_target_pairs={{96,0},{0,32},{32,64},{64,96},{97,1},{1,33},{33,65},{65,97},{98,2}... | collective-permute-start | bytes 786440 | tf_op jit(solution)/shard_map/ppermute | solution.py:34
  98.0 14.6 %collective-permute-start.26 = (bf16[2,256,256]{2,1,0:T(8,128)(2,1)S(1)}, bf16[2,256,256]{2,1,0:T(8,128)(2,1)S(1)}, u32[]{:S(2)}, u32[]{:S(2)}) collective-permute-start(bf16[2,256,256]{2,1,0:T(8,128)(2,1)S(1)} %pack.11.refs_0_), channel_id=1, source_target_pairs={{32,0},{64,32},{96,64},{0,96},{33,1},{65,33},{97,65},{1,97},{34,2}... | collective-permute-start | bytes 786440 | tf_op jit(solution)/shard_map/ppermute | solution.py:34
  113.7 14.7 %collective-permute-start.35 = (bf16[4,256,256]{2,1,0:T(8,128)(2,1)S(1)}, bf16[4,256,256]{2,1,0:T(8,128)(2,1)S(1)}, u32[]{:S(2)}, u32[]{:S(2)}) collective-permute-start(bf16[4,256,256]{2,1,0:T(8,128)(2,1)S(1)} %pack.12.refs_0_), channel_id=1, source_target_pairs={{3,0},{0,1},{1,2},{2,3},{7,4},{4,5},{5,6},{6,7},{11,8},{8,9},{9,10... | collective-permute-start | bytes 1572872 | tf_op jit(solution)/shard_map/ppermute | solution.py:34
  113.7 16.5 %collective-permute-start.34 = (bf16[4,256,256]{2,1,0:T(8,128)(2,1)S(1)}, bf16[4,256,256]{2,1,0:T(8,128)(2,1)S(1)}, u32[]{:S(2)}, u32[]{:S(2)}) collective-permute-start(bf16[4,256,256]{2,1,0:T(8,128)(2,1)S(1)} %pack.12.refs_0_), channel_id=1, source_target_pairs={{1,0},{2,1},{3,2},{0,3},{5,4},{6,5},{7,6},{4,7},{9,8},{10,9},{11,1... | collective-permute-start | bytes 1572872 | tf_op jit(solution)/shard_map/ppermute | solution.py:34
  117.6 12.5 %collective-permute-start.38 = (bf16[256,256]{1,0:T(8,128)(2,1)S(1)}, bf16[256,256]{1,0:T(8,128)(2,1)S(1)}, u32[]{:S(2)}, u32[]{:S(2)}) collective-permute-start(bf16[256,256]{1,0:T(8,128)(2,1)S(1)} %product.3.refs_0_.prod_ref), channel_id=1, source_target_pairs={{128,0},{0,128},{129,1},{1,129},{130,2},{2,130},{131,3},{3,131},{1... | collective-permute-start | bytes 393224 | tf_op jit(solution)/shard_map/ppermute | solution.py:34
  117.8 16.0 %collective-permute-start.33 = (bf16[256,256]{1,0:T(8,128)(2,1)S(1)}, bf16[256,256]{1,0:T(8,128)(2,1)S(1)}, u32[]{:S(2)}, u32[]{:S(2)}) collective-permute-start(bf16[256,256]{1,0:T(8,128)(2,1)S(1)} %product.3.refs_0_.prod_ref), channel_id=1, source_target_pairs={{0,0},{1,16},{2,32},{3,48},{4,64},{5,80},{6,96},{7,112},{8,128},{9... | collective-permute-start | bytes 393224 | tf_op jit(solution)/shard_map/ppermute | solution.py:38
  131.1 14.5 %collective-permute-start.40 = (bf16[2,256,256]{2,1,0:T(8,128)(2,1)S(1)}, bf16[2,256,256]{2,1,0:T(8,128)(2,1)S(1)}, u32[]{:S(2)}, u32[]{:S(2)}) collective-permute-start(bf16[2,256,256]{2,1,0:T(8,128)(2,1)S(1)} %pack.13.refs_0_), channel_id=1, source_target_pairs={{96,0},{0,32},{32,64},{64,96},{97,1},{1,33},{33,65},{65,97},{98,2}... | collective-permute-start | bytes 786440 | tf_op jit(solution)/shard_map/ppermute | solution.py:34
  131.5 14.1 %collective-permute-start.39 = (bf16[2,256,256]{2,1,0:T(8,128)(2,1)S(1)}, bf16[2,256,256]{2,1,0:T(8,128)(2,1)S(1)}, u32[]{:S(2)}, u32[]{:S(2)}) collective-permute-start(bf16[2,256,256]{2,1,0:T(8,128)(2,1)S(1)} %pack.13.refs_0_), channel_id=1, source_target_pairs={{32,0},{64,32},{96,64},{0,96},{33,1},{65,33},{97,65},{1,97},{34,2}... | collective-permute-start | bytes 786440 | tf_op jit(solution)/shard_map/ppermute | solution.py:34
  133.8 11.9 %collective-permute-start.36 = (bf16[2,256,256]{2,1,0:T(8,128)(2,1)S(1)}, bf16[2,256,256]{2,1,0:T(8,128)(2,1)S(1)}, u32[]{:S(2)}, u32[]{:S(2)}) collective-permute-start(bf16[2,256,256]{2,1,0:T(8,128)(2,1)S(1)} %get-tuple-element.34), channel_id=1, source_target_pairs={{1,0},{2,1},{3,2},{0,3},{5,4},{6,5},{7,6},{4,7},{9,8},{10,9},{11,1... | collective-permute-start | bytes 786440 | tf_op jit(solution)/shard_map/ppermute | solution.py:34
  (21 other events, 155.9 us)
